TPU v7x, 32 devices: a whole 2x2x4 slice. The times are simulated.
32 devices in a mesh: row: 4 (over x, core), col: 8 (over z, y).
Axes of the slice: x: 2, y: 2, z: 4, core: 2. Of those that a mesh axis runs over, the one named last changes fastest.
Arguments:
- heights: float32 [1024, 2048], P('row', 'col'), may hold values from -2 to 2
- shadow: int32 [1024, 2048], P('row', 'col'), may hold values 0 or 1
- image_tiles: bfloat16 [2048, 256, 256], P(('row', 'col')), may hold values from 0.019897461 to 0.59765625
- image_dest: int32 [2048, 1], P(('row', 'col')), may hold values from 0 to 31; in each aligned block of 64 rows (0 to 63, 64 to 127, ...) at most 4 rows name the same one
- sun_gain: bfloat16 [2048, 4], P(('row', 'col')), may hold values from -1 to 2.5, as said below
- shot_dest: int32 [8192, 1], P(('row', 'col')), may hold values from 0 to 31; in each aligned block of 256 rows (0 to 255, 256 to 511, ...) at most 16 rows name the same one
- shot_pixel: int32 [8192], P(('row', 'col')), may hold values from 0 to 65535
- shot_height: float32 [8192], P(('row', 'col')), may hold values from -2 to 2
Outputs:
- surface: float32 [1024, 2048], P('row', 'col')
Inputs may be any that keep to these rules, and one draw needn't show every extreme that they name: `image_dest`: among one device's 64 image tiles, no tile owner is named more than 4 times. `shot_dest`: among one device's 256 laser shots, no tile owner is named more than 16 times. `sun_gain`: each row is a unit sun direction with elevation between 0.02 and 0.35 radians, followed by a gain between 0.4 and 2.5.
All inputs are finite; a program needn't handle non-finite values. No bound on the sum of `shadow` on one device may be relied on, other than what follows from the above.
Results may differ from a plain program's by a relative error of at most 0.0015.
Values may be sent and summed in bfloat16 or wider, within the bound.
A program may use at most 256 MiB of HBM per device.

v0:
```python
import jax
import jax.numpy as jnp
from jax import lax
from jax.sharding import PartitionSpec as P

ITERS = 2


sharpness = 8.0
step_size = 0.01
smooth_weight = 2.0
laser_weight = 20.0


def with_halo(value, sides, width):
    for axis, dim in sides:
        devices, length = (lax.axis_size(axis), value.shape[dim])
        up = [(i, (i + 1) % devices) for i in range(devices - 1)]
        down = [(j, i) for i, j in up]
        last = lax.slice_in_dim(value, length - width, length, axis=dim)
        initial = lax.slice_in_dim(value, 0, width, axis=dim)
        before = lax.ppermute(last, axis, up)
        after = lax.ppermute(initial, axis, down)
        value = jnp.concatenate([before, value, after], axis=dim)
    return value


def slot_places(targets, capacity):
    length = targets.shape[0]
    before = jnp.arange(length)[None, :] < jnp.arange(length)[:, None]
    alike = targets[None, :] == targets[:, None]
    order_rank = jnp.sum(jnp.logical_and(before, alike), axis=1)
    return targets * capacity + order_rank


def surface_terms(padded, center):
    slope_x = (padded[1:-1, 2:] - padded[1:-1, :-2]) * 0.5
    slope_y = (padded[2:, 1:-1] - padded[:-2, 1:-1]) * 0.5
    laplace = (
        padded[2:, 1:-1] + padded[:-2, 1:-1] + padded[1:-1, 2:] + padded[1:-1, :-2] - 4.0 * center
    )
    return (slope_x, slope_y, laplace)


def image_terms(slope_x, slope_y, pieces, angles):
    sun_x = angles[:, 0, None, None]
    sun_y = angles[:, 1, None, None]
    sun_z = angles[:, 2, None, None]
    gain = angles[:, 3, None, None]
    inverse = lax.rsqrt(1.0 + slope_x * slope_x + slope_y * slope_y)
    cosine = (sun_z - slope_x * sun_x - slope_y * sun_y) * inverse
    refl = jax.nn.softplus(sharpness * cosine) / sharpness
    sigma = jax.nn.sigmoid(sharpness * cosine)
    along_x = -sun_x * inverse - cosine * slope_x * inverse * inverse
    along_y = -sun_y * inverse - cosine * slope_y * inverse * inverse
    observed = pieces.astype(jnp.float32)
    seen = gain * observed * sigma
    model = gain * gain * refl * sigma
    return (
        seen * along_x,
        seen * along_y,
        model * along_x,
        model * along_y,
        gain * observed * refl,
        gain * gain * refl * refl,
    )


def body(heights, shadow, image_tiles, image_dest, sun_gain, shot_dest, shot_pixel, shot_height):
    row_count = lax.axis_size("row")
    col_count = lax.axis_size("col")
    devices = row_count * col_count
    tile_side = heights.shape[0]
    image_count = image_dest.shape[0]
    image_cap = max(2, 2 * image_count // devices)
    slot_total = devices * image_cap
    places = slot_places(image_dest[:, 0], image_cap)
    send_pixels = (
        jnp.zeros((slot_total, tile_side, tile_side), jnp.bfloat16).at[places].set(image_tiles)
    )
    send_angles = jnp.zeros((slot_total, 4), jnp.bfloat16).at[places].set(sun_gain)
    got_pixels, got_angles = (
        lax.all_to_all(send_pixels, ("row", "col"), split_axis=0, concat_axis=0, tiled=True),
        lax.all_to_all(send_angles, ("row", "col"), split_axis=0, concat_axis=0, tiled=True),
    )
    shot_count = shot_dest.shape[0]
    shot_cap = max(2, 2 * shot_count // devices)
    shot_slots = slot_places(shot_dest[:, 0], shot_cap)
    record = jnp.stack([shot_height, jnp.ones_like(shot_height)], axis=1)
    send_record = jnp.zeros((devices * shot_cap, 2), jnp.float32).at[shot_slots].set(record)
    send_where = jnp.zeros((devices * shot_cap,), jnp.int32).at[shot_slots].set(shot_pixel)
    got_record, got_where = (
        lax.all_to_all(send_record, ("row", "col"), split_axis=0, concat_axis=0, tiled=True),
        lax.all_to_all(send_where, ("row", "col"), split_axis=0, concat_axis=0, tiled=True),
    )
    cells = tile_side * tile_side
    hits = (
        jnp.zeros((cells,), jnp.float32)
        .at[got_where]
        .add(got_record[:, 1])
        .reshape(tile_side, tile_side)
    )
    height_sum = (
        jnp.zeros((cells,), jnp.float32)
        .at[got_where]
        .add(got_record[:, 1] * got_record[:, 0])
        .reshape(tile_side, tile_side)
    )
    lit = 1.0 - shadow.astype(jnp.float32)
    block = 32
    groups = slot_total // block
    grouped_pixels = got_pixels.reshape(groups, block, tile_side, tile_side)
    grouped_angles = got_angles.astype(jnp.float32).reshape(groups, block, 4)
    surface = heights
    for sweep in range(ITERS):
        padded = with_halo(surface, (("row", 0), ("col", 1)), 1)
        slope_x, slope_y, laplace = surface_terms(padded, surface)

        def accumulate(carry, group):
            pieces, angles = group
            terms = image_terms(slope_x, slope_y, pieces, angles)
            return (
                tuple((total + jnp.sum(term, axis=0) for total, term in zip(carry, terms))),
                None,
            )

        start = tuple((jnp.zeros((tile_side, tile_side), jnp.float32) for member in range(6)))
        totals, unused = lax.scan(accumulate, start, (grouped_pixels, grouped_angles))
        obs_x, obs_y, fit_x, fit_y, cross, power = totals
        global_cross, global_power = lax.psum(
            (jnp.sum(lit * cross), jnp.sum(lit * power)), ("row", "col")
        )
        albedo = global_cross / global_power
        grad_x = lit * (albedo * albedo * fit_x - albedo * obs_x)
        grad_y = lit * (albedo * albedo * fit_y - albedo * obs_y)
        rims = with_halo(
            jnp.stack([grad_x, grad_y]).astype(jnp.bfloat16), (("row", 1), ("col", 2)), 1
        ).astype(jnp.float32)
        pad_x = rims[0]
        pad_y = rims[1]
        data = (pad_x[1:-1, :-2] - pad_x[1:-1, 2:]) * 0.5 + (
            pad_y[:-2, 1:-1] - pad_y[2:, 1:-1]
        ) * 0.5
        surface = surface - step_size * (
            data - smooth_weight * laplace + laser_weight * (hits * surface - height_sum)
        )
    return surface


def solution(mesh):
    placed = (
        P("row", "col"),
        P("row", "col"),
        P(("row", "col"), None, None),
        P(("row", "col"), None),
        P(("row", "col"), None),
        P(("row", "col"), None),
        P(("row", "col")),
        P(("row", "col")),
    )
    return jax.shard_map(
        body, mesh=mesh, in_specs=placed, out_specs=P("row", "col"), check_vma=False
    )
```

profile of v0, /device:TPU:0, one launch (start us, length us, event | category | flops | bytes accessed | tf_op | source)
XLA Modules:
  0.0 745.6 jit_solution(17454001105515229772)
XLA Ops:
  4.1 7.3 all-to-all-start
  13.0 1.6 scatter_custom_fusion.2
  15.2 3.3 all-to-all-done
  18.5 2.6 all-to-all-start.2
  21.1 5.9 broadcast_in_dim.7
  27.0 22.1 %scatter_fusion = bf16[128,256,256]{2,1,0:T(8,128)(2,1)} fusion(bf16[128,256,256]{2,1,0:T(8,128)(2,1)} %broadcast_in_dim.7, s32[64]{0:T(128)S(1)} %fusion.41, bf16[64,256,256]{2,1,0:T(8,128)(2,1)} %param.14), kind=kCustom, calls=%fused_computation.1 | custom fusion | bytes 25166080 | tf_op jit(solution)/shard_map/scatter | solution.py:79
  49.2 6.0 all-to-all-start.1
  55.2 2.1 collective-permute-start
  57.3 1.3 collective-permute-start.1
  58.6 2.9 collective-permute-done.1
  61.6 1.3 collective-permute-start.2
  62.9 4.6 collective-permute-start.3
  67.7 1.2 scatter_custom_fusion.3
  70.1 66.1 %collective-permute-done.2 = f32[258,1]{1,0:T(8,128)S(1)} collective-permute-done((f32[258,1]{1,0:T(8,128)S(1)}, f32[258,1]{1,0:T(8,128)S(1)}, u32[]{:S(2)}, u32[]{:S(2)}) %collective-permute-start.2) | collective-permute-done | bytes 1064 | tf_op jit(solution)/shard_map/ppermute | solution.py:23
  136.2 10.9 %collective-permute-done.3 = f32[258,1]{1,0:T(8,128)S(1)} collective-permute-done((f32[258,1]{1,0:T(8,128)S(1)}, f32[258,1]{1,0:T(8,128)S(1)}, u32[]{:S(2)}, u32[]{:S(2)}) %collective-permute-start.3) | collective-permute-done | bytes 1064 | tf_op jit(solution)/shard_map/ppermute | solution.py:22
  149.8 280.6 %all-to-all-done.1 = bf16[128,256,256]{2,1,0:T(8,128)(2,1)} async-done(((bf16[128,256,256]{2,1,0:T(8,128)(2,1)}), bf16[128,256,256]{2,1,0:T(8,128)(2,1)}, u32[]{:S(2)}, u32[]{:S(2)}) %all-to-all-start.1) | async-done | bytes 16777248 | tf_op jit(solution)/shard_map/all_to_all | solution.py:83
  430.4 3.3 all-to-all-start.3
  433.7 80.7 %while.44 = (s32[]{:T(128)}, f32[256,256]{1,0:T(8,128)S(1)}, f32[256,256]{1,0:T(8,128)S(1)}, f32[256,256]{1,0:T(8,128)S(1)}, f32[256,256]{1,0:T(8,128)S(1)}, /*i...) while((s32[]{:T(128)}, f32[256,256]{1,0:T(8,128)S(1)}, ...), condition=%wide.region_10.11_spmd.clone, body=%wide.region_3.10_spmd.clone.sunk | while | flops 90701952 | bytes 12062497 | solution.py:128
  433.8 18.6 %fusion.51 = (f32[256,256]{1,0:T(8,128)S(1)}, f32[256,256]{1,0:T(8,128)S(1)}, f32[256,256]{1,0:T(8,128)S(1)}, f32[256,256]{1,0:T(8,128)S(1)}, f32[256,256]{1,0:T(8,128)S(1)}, /*index=5*/f32[256,256]{1,0:T(8,128)}) fusion(f32[256,256]{1,0:T(8,128)S(1)} %rsqrt_bitcast_fusion.4, f32[32]{0:T(128)S(1)} %get-tuple-element.780, ...), kind=kLoop, calls=%fused_computation.10.clone.1 | loop fusion | flops 89784320 | bytes 6554500 | tf_op jit(solution)/shard_map/while/body/eval_jaxpr/reduce_sum | solution.py:123
  452.4 1.1 select_add_fusion.20
  454.0 18.6 %fusion.51 = (f32[256,256]{1,0:T(8,128)S(1)}, f32[256,256]{1,0:T(8,128)S(1)}, f32[256,256]{1,0:T(8,128)S(1)}, f32[256,256]{1,0:T(8,128)S(1)}, f32[256,256]{1,0:T(8,128)S(1)}, /*index=5*/f32[256,256]{1,0:T(8,128)}) fusion(f32[256,256]{1,0:T(8,128)S(1)} %rsqrt_bitcast_fusion.4, f32[32]{0:T(128)S(1)} %get-tuple-element.780, ...), kind=kLoop, calls=%fused_computation.10.clone.1 | loop fusion | flops 89784320 | bytes 6554500 | tf_op jit(solution)/shard_map/while/body/eval_jaxpr/reduce_sum | solution.py:123
  472.6 1.1 select_add_fusion.20
  474.1 18.6 %fusion.51 = (f32[256,256]{1,0:T(8,128)S(1)}, f32[256,256]{1,0:T(8,128)S(1)}, f32[256,256]{1,0:T(8,128)S(1)}, f32[256,256]{1,0:T(8,128)S(1)}, f32[256,256]{1,0:T(8,128)S(1)}, /*index=5*/f32[256,256]{1,0:T(8,128)}) fusion(f32[256,256]{1,0:T(8,128)S(1)} %rsqrt_bitcast_fusion.4, f32[32]{0:T(128)S(1)} %get-tuple-element.780, ...), kind=kLoop, calls=%fused_computation.10.clone.1 | loop fusion | flops 89784320 | bytes 6554500 | tf_op jit(solution)/shard_map/while/body/eval_jaxpr/reduce_sum | solution.py:123
  492.8 1.1 select_add_fusion.20
  494.3 18.6 %fusion.51 = (f32[256,256]{1,0:T(8,128)S(1)}, f32[256,256]{1,0:T(8,128)S(1)}, f32[256,256]{1,0:T(8,128)S(1)}, f32[256,256]{1,0:T(8,128)S(1)}, f32[256,256]{1,0:T(8,128)S(1)}, /*index=5*/f32[256,256]{1,0:T(8,128)}) fusion(f32[256,256]{1,0:T(8,128)S(1)} %rsqrt_bitcast_fusion.4, f32[32]{0:T(128)S(1)} %get-tuple-element.780, ...), kind=kLoop, calls=%fused_computation.10.clone.1 | loop fusion | flops 89784320 | bytes 6554500 | tf_op jit(solution)/shard_map/while/body/eval_jaxpr/reduce_sum | solution.py:123
  513.0 1.1 select_add_fusion.20
  514.4 1.7 multiply_reduce_fusion.12
  516.1 40.7 %all-reduce.2 = (f32[]{:T(128)}, f32[]{:T(128)}) all-reduce(f32[]{:T(128)} %get-tuple-element.476, f32[]{:T(128)} %get-tuple-element.475), channel_id=1, replica_groups=mesh['row'=4,'col'=8] {'row','col'}, use_global_device_ids=true, to_apply=%region_12.13 | all-reduce | flops 2 | bytes 16 | tf_op jit(solution)/shard_map/psum | solution.py:130
  558.2 1.1 fusion.25
  559.2 1.3 collective-permute-start.4
  560.5 1.3 collective-permute-start.5
  563.3 2.8 collective-permute-done.5
  566.3 2.7 collective-permute-start.6
  569.0 1.5 collective-permute-start.7
  570.5 3.4 scatter_custom_fusion.4
  573.9 3.4 scatter_custom_fusion.5
  578.4 3.9 collective-permute-start.8
  582.3 1.3 collective-permute-start.9
  583.6 2.0 collective-permute-done.9
  585.7 1.3 collective-permute-start.10
  587.0 5.1 collective-permute-start.11
  592.3 1.0 collective-permute-done.10
  593.2 4.6 collective-permute-done.11
  597.9 1.0 multiply_bitcast_fusion
  598.8 80.8 %while.45 = (s32[]{:T(128)}, f32[256,256]{1,0:T(8,128)S(1)}, f32[256,256]{1,0:T(8,128)S(1)}, f32[256,256]{1,0:T(8,128)S(1)}, f32[256,256]{1,0:T(8,128)S(1)}, /*i...) while((s32[]{:T(128)}, f32[256,256]{1,0:T(8,128)S(1)}, ...), condition=%wide.region_27.28_spmd.clone, body=%wide.region_20.27_spmd.clone.sunk | while | flops 90701952 | bytes 12062497 | solution.py:128
  598.9 18.7 %fusion.52 = (f32[256,256]{1,0:T(8,128)S(1)}, f32[256,256]{1,0:T(8,128)S(1)}, f32[256,256]{1,0:T(8,128)S(1)}, f32[256,256]{1,0:T(8,128)S(1)}, f32[256,256]{1,0:T(8,128)S(1)}, /*index=5*/f32[256,256]{1,0:T(8,128)}) fusion(f32[256,256]{1,0:T(8,128)S(1)} %rsqrt_bitcast_fusion.5, f32[32]{0:T(128)S(1)} %get-tuple-element.812, ...), kind=kLoop, calls=%fused_computation.41.clone.1 | loop fusion | flops 89784320 | bytes 6554500 | tf_op jit(solution)/shard_map/while/body/eval_jaxpr/reduce_sum | solution.py:123
  617.6 1.1 select_add_fusion.23
  619.1 18.7 %fusion.52 = (f32[256,256]{1,0:T(8,128)S(1)}, f32[256,256]{1,0:T(8,128)S(1)}, f32[256,256]{1,0:T(8,128)S(1)}, f32[256,256]{1,0:T(8,128)S(1)}, f32[256,256]{1,0:T(8,128)S(1)}, /*index=5*/f32[256,256]{1,0:T(8,128)}) fusion(f32[256,256]{1,0:T(8,128)S(1)} %rsqrt_bitcast_fusion.5, f32[32]{0:T(128)S(1)} %get-tuple-element.812, ...), kind=kLoop, calls=%fused_computation.41.clone.1 | loop fusion | flops 89784320 | bytes 6554500 | tf_op jit(solution)/shard_map/while/body/eval_jaxpr/reduce_sum | solution.py:123
  637.8 1.1 select_add_fusion.23
  639.4 18.7 %fusion.52 = (f32[256,256]{1,0:T(8,128)S(1)}, f32[256,256]{1,0:T(8,128)S(1)}, f32[256,256]{1,0:T(8,128)S(1)}, f32[256,256]{1,0:T(8,128)S(1)}, f32[256,256]{1,0:T(8,128)S(1)}, /*index=5*/f32[256,256]{1,0:T(8,128)}) fusion(f32[256,256]{1,0:T(8,128)S(1)} %rsqrt_bitcast_fusion.5, f32[32]{0:T(128)S(1)} %get-tuple-element.812, ...), kind=kLoop, calls=%fused_computation.41.clone.1 | loop fusion | flops 89784320 | bytes 6554500 | tf_op jit(solution)/shard_map/while/body/eval_jaxpr/reduce_sum | solution.py:123
  658.0 1.1 select_add_fusion.23
  659.6 18.7 %fusion.52 = (f32[256,256]{1,0:T(8,128)S(1)}, f32[256,256]{1,0:T(8,128)S(1)}, f32[256,256]{1,0:T(8,128)S(1)}, f32[256,256]{1,0:T(8,128)S(1)}, f32[256,256]{1,0:T(8,128)S(1)}, /*index=5*/f32[256,256]{1,0:T(8,128)}) fusion(f32[256,256]{1,0:T(8,128)S(1)} %rsqrt_bitcast_fusion.5, f32[32]{0:T(128)S(1)} %get-tuple-element.812, ...), kind=kLoop, calls=%fused_computation.41.clone.1 | loop fusion | flops 89784320 | bytes 6554500 | tf_op jit(solution)/shard_map/while/body/eval_jaxpr/reduce_sum | solution.py:123
  678.2 1.1 select_add_fusion.23
  679.7 1.6 multiply_reduce_fusion.10
  681.3 41.1 %all-reduce.1 = (f32[]{:T(128)}, f32[]{:T(128)}) all-reduce(f32[]{:T(128)} %get-tuple-element.474, f32[]{:T(128)} %get-tuple-element.473), channel_id=1, replica_groups=mesh['row'=4,'col'=8] {'row','col'}, use_global_device_ids=true, to_apply=%region_29.30 | all-reduce | flops 2 | bytes 16 | tf_op jit(solution)/shard_map/psum | solution.py:130
  723.7 1.1 fusion.27
  724.8 1.3 collective-permute-start.12
  726.1 1.3 collective-permute-start.13
  727.4 4.3 collective-permute-done.13
  731.9 3.2 collective-permute-start.14
  735.0 1.3 collective-permute-start.15
  736.3 1.2 collective-permute-done.14
  737.6 4.7 collective-permute-done.15
  742.6 3.0 fusion.17
  (134 shorter events, 16.8 us)
Async XLA Ops:
  4.1 14.5 %all-to-all-start = ((bf16[32,4,4]{1,2,0:T(4,128)(2,1)}), bf16[32,4,4]{1,2,0:T(4,128)(2,1)S(1)}, u32[]{:S(2)}, u32[]{:S(2)}) async-start(bf16[32,4,4]{1,2,0:T(4,128)(2,1)} %copy.40), calls=%async_computation | async-start | bytes 65536 | tf_op jit(solution)/shard_map/all_to_all | solution.py:84
  18.5 30.7 %all-to-all-start.2 = ((s32[32,16,1]{1,2,0:T(1,128)}), s32[32,16,1]{1,2,0:T(1,128)S(1)}, u32[]{:S(2)}, u32[]{:S(2)}) async-start(s32[32,16,1]{1,2,0:T(1,128)} %bitcast.14), calls=%async_computation.2 | async-start | bytes 32768 | tf_op jit(solution)/shard_map/all_to_all | solution.py:94
  49.2 6.0 copy-start.1
  49.2 18.3 %copy-start.11 = (f32[256]{0:T(256)S(1)}, f32[256]{0:T(256)}, u32[]{:S(2)}) copy-start(f32[256]{0:T(256)} %param.19) | copy-start | bytes 3076
  49.2 381.2 %all-to-all-start.1 = ((bf16[128,256,256]{2,1,0:T(8,128)(2,1)}), bf16[128,256,256]{2,1,0:T(8,128)(2,1)}, u32[]{:S(2)}, u32[]{:S(2)}) async-start(bf16[128,256,256]{2,1,0:T(8,128)(2,1)} %scatter_fusion), calls=%async_computation.1 | async-start | bytes 33554432 | tf_op jit(solution)/shard_map/all_to_all | solution.py:83
  55.2 3.4 collective-permute-start
  57.3 4.2 collective-permute-start.1
  61.5 372.2 %copy-start.8 = (f32[1,256]{1,0:T(1,128)}, f32[1,256]{1,0:T(1,128)S(1)}, u32[]{:S(2)}) copy-start(f32[1,256]{1,0:T(1,128)S(1)} %collective-permute-done.1) | copy-start | bytes 3076
  61.6 74.7 %collective-permute-start.2 = (f32[258,1]{1,0:T(8,128)S(1)}, f32[258,1]{1,0:T(8,128)S(1)}, u32[]{:S(2)}, u32[]{:S(2)}) collective-permute-start(f32[258,1]{1,0:T(8,128)S(1)} %get-tuple-element.577), channel_id=1, source_target_pairs={{1,0},{2,1},{3,2},{4,3},{5,4},{6,5},{7,6},{9,8},{10,9},{11,10},{12... | collective-permute-start | bytes 3104 | tf_op jit(solution)/shard_map/ppermute | solution.py:23
  62.9 84.2 %collective-permute-start.3 = (f32[258,1]{1,0:T(8,128)S(1)}, f32[258,1]{1,0:T(8,128)S(1)}, u32[]{:S(2)}, u32[]{:S(2)}) collective-permute-start(f32[258,1]{1,0:T(8,128)S(1)} %get-tuple-element.578), channel_id=1, source_target_pairs={{0,1},{1,2},{2,3},{3,4},{4,5},{5,6},{6,7},{8,9},{9,10},{10,11},{11... | collective-permute-start | bytes 3104 | tf_op jit(solution)/shard_map/ppermute | solution.py:22
  147.1 286.5 %copy-start.5 = (f32[258,1]{1,0:T(8,128)}, f32[258,1]{1,0:T(8,128)S(1)}, u32[]{:S(2)}) copy-start(f32[258,1]{1,0:T(8,128)S(1)} %collective-permute-done.3) | copy-start | bytes 3100
  430.4 132.1 %all-to-all-start.3 = ((f32[32,16,2]{1,2,0:T(2,128)}), f32[32,16,2]{1,2,0:T(2,128)}, u32[]{:S(2)}, u32[]{:S(2)}) async-start(f32[32,16,2]{1,2,0:T(2,128)} %copy.47), calls=%async_computation.3 | async-start | bytes 65536 | tf_op jit(solution)/shard_map/all_to_all | solution.py:93
  514.4 63.4 %copy-start.2 = (f32[256,256]{1,0:T(8,128)S(1)}, f32[256,256]{1,0:T(8,128)}, u32[]{:S(2)}) copy-start(f32[256,256]{1,0:T(8,128)} %param.12) | copy-start | bytes 786436
  514.4 63.4 %copy-start.6 = (f32[258,1]{1,0:T(8,128)S(1)}, f32[258,1]{1,0:T(8,128)}, u32[]{:S(2)}) copy-start(f32[258,1]{1,0:T(8,128)} %copy-done.5) | copy-start | bytes 3100
  514.4 63.4 %copy-start.9 = (f32[1,256]{1,0:T(1,128)S(1)}, f32[1,256]{1,0:T(1,128)}, u32[]{:S(2)}) copy-start(f32[1,256]{1,0:T(1,128)} %copy-done.8) | copy-start | bytes 3076
  559.2 4.1 collective-permute-start.4
  560.5 5.6 collective-permute-start.5
  566.3 11.2 %collective-permute-start.6 = (bf16[2,258,1]{2,1,0:T(8,128)(2,1)S(1)}, bf16[2,258,1]{2,1,0:T(8,128)(2,1)S(1)}, u32[]{:S(2)}, u32[]{:S(2)}) collective-permute-start(bf16[2,258,1]{2,1,0:T(8,128)(2,1)S(1)} %get-tuple-element.575), channel_id=1, source_target_pairs={{0,1},{1,2},{2,3},{3,4},{4,5},{5,6},{6,7},{8,9},{9,10},{10,11},{11... | collective-permute-start | bytes 3104 | tf_op jit(solution)/shard_map/ppermute | solution.py:22
  569.0 8.5 %collective-permute-start.7 = (bf16[2,258,1]{2,1,0:T(8,128)(2,1)S(1)}, bf16[2,258,1]{2,1,0:T(8,128)(2,1)S(1)}, u32[]{:S(2)}, u32[]{:S(2)}) collective-permute-start(bf16[2,258,1]{2,1,0:T(8,128)(2,1)S(1)} %get-tuple-element.576), channel_id=1, source_target_pairs={{1,0},{2,1},{3,2},{4,3},{5,4},{6,5},{7,6},{9,8},{10,9},{11,10},{12... | collective-permute-start | bytes 3104 | tf_op jit(solution)/shard_map/ppermute | solution.py:23
  577.4 15.9 %copy-start.3 = (f32[256,256]{1,0:T(8,128)}, f32[256,256]{1,0:T(8,128)S(1)}, u32[]{:S(2)}) copy-start(f32[256,256]{1,0:T(8,128)S(1)} %reshape.155) | copy-start | bytes 786436
  577.5 14.7 %copy-start.4 = (f32[256,256]{1,0:T(8,128)}, f32[256,256]{1,0:T(8,128)S(1)}, u32[]{:S(2)}) copy-start(f32[256,256]{1,0:T(8,128)S(1)} %reshape.154) | copy-start | bytes 786436
  578.4 20.5 %copy-start = (f32[256,256]{1,0:T(8,128)}, f32[256,256]{1,0:T(8,128)S(1)}, u32[]{:S(2)}) copy-start(f32[256,256]{1,0:T(8,128)S(1)} %fusion.23) | copy-start | bytes 786436
  578.4 5.2 collective-permute-start.8
  582.3 3.3 collective-permute-start.9
  585.6 13.2 %copy-start.10 = (f32[1,256]{1,0:T(1,128)}, f32[1,256]{1,0:T(1,128)S(1)}, u32[]{:S(2)}) copy-start(f32[1,256]{1,0:T(1,128)S(1)} %collective-permute-done.9) | copy-start | bytes 3076
  585.7 7.5 %collective-permute-start.10 = (f32[258,1]{1,0:T(8,128)S(1)}, f32[258,1]{1,0:T(8,128)S(1)}, u32[]{:S(2)}, u32[]{:S(2)}) collective-permute-start(f32[258,1]{1,0:T(8,128)S(1)} %get-tuple-element.573), channel_id=1, source_target_pairs={{1,0},{2,1},{3,2},{4,3},{5,4},{6,5},{7,6},{9,8},{10,9},{11,10},{12... | collective-permute-start | bytes 3104 | tf_op jit(solution)/shard_map/ppermute | solution.py:23
  587.0 10.8 %collective-permute-start.11 = (f32[258,1]{1,0:T(8,128)S(1)}, f32[258,1]{1,0:T(8,128)S(1)}, u32[]{:S(2)}, u32[]{:S(2)}) collective-permute-start(f32[258,1]{1,0:T(8,128)S(1)} %get-tuple-element.574), channel_id=1, source_target_pairs={{0,1},{1,2},{2,3},{3,4},{4,5},{5,6},{6,7},{8,9},{9,10},{10,11},{11... | collective-permute-start | bytes 3104 | tf_op jit(solution)/shard_map/ppermute | solution.py:22
  597.9 1.0 copy-start.7
  724.8 2.6 collective-permute-start.12
  726.1 5.6 collective-permute-start.13
  731.9 5.7 collective-permute-start.14
  735.0 7.2 collective-permute-start.15
where the time goes:
time: 748 us; the launch traced here: 746 us
  waiting for transfers between devices  384 us (51%)
  other arithmetic  184 us (25%)
  blocking collectives  81.8 us (11%)
  starting transfers between devices  53.8 us (7%)
  local copies, waits for them, and re-layouts  38.1 us (5%)
    all_to_all x1, waiting for transfers between devices, body(): lax.all_to_all(send_pixels, ('row', 'col'), split_axis=0, concat_axis=0,...  281 us
    reduce_sum x8, other arithmetic, accumulate(): jnp.sum(term, axis=0)  149 us
    ppermute x8, waiting for transfers between devices, with_halo(): after = lax.ppermute(initial, axis, down)  83.7 us
    psum x2, blocking collectives, body(): lax.psum((jnp.sum(lit * cross), jnp.sum(lit * power)), ('row', 'col'))  81.8 us
    ppermute x8, starting transfers between devices, with_halo(): before = lax.ppermute(last, axis, up)  24.2 us
    scatter x1, local copies, waits for them, and re-layouts, body(): jnp.zeros((slot_total, tile_side, tile_side), jnp.bfloat16).at[places]  22.1 us
    ppermute x8, waiting for transfers between devices, with_halo(): before = lax.ppermute(last, axis, up)  16.7 us
  transfers between devices with their start and end apart: 20, of which 12 were waited for; matrix products, arithmetic and copies ran while one was open for 17% of the time, Pallas kernels for 0%

commit v1 on v0

v1 whole, which is shorter than its diff:
```python
import functools
import math

import jax
import jax.numpy as jnp
from jax import lax
from jax.experimental import pallas as pl
from jax.experimental.pallas import tpu as pltpu
from jax.sharding import PartitionSpec as P

ITERS = 2

sharpness = 8.0
step_size = 0.01
smooth_weight = 2.0
laser_weight = 20.0

AXES = ("row", "col")
LOG2E = math.log2(math.e)
CHUNK = 16
LINK = jnp.float32


def rim_specs(side, cols, tiles, tile_of):
    def at(offset, block, where):
        def index(*args):
            tile = jnp.clip(tile_of(*args) + offset, 0, tiles - 1)
            return (tile,) + where

        return pl.BlockSpec((1,) + block, index)

    return [
        at(0, (side, side), (0, 0)),
        at(-cols, (8, side), (side // 8 - 1, 0)),
        at(cols, (8, side), (0, 0)),
        at(-1, (side, 128), (0, side // 128 - 1)),
        at(1, (side, 128), (0, 0)),
    ]


def edges(tile, rows, cols):
    row, col = tile // cols, lax.rem(tile, cols)
    as_gate = lambda test: jnp.where(test, 1.0, 0.0).astype(jnp.float32)
    return as_gate(row > 0), as_gate(row < rows - 1), as_gate(col > 0), as_gate(col < cols - 1)


def shifted(center, up, down, left, right):
    side = center.shape[0]
    row = lax.broadcasted_iota(jnp.int32, center.shape, 0)
    col = lax.broadcasted_iota(jnp.int32, center.shape, 1)
    above = jnp.where(row == 0, up, pltpu.roll(center, 1, 0))
    below = jnp.where(row == side - 1, down, pltpu.roll(center, side - 1, 0))
    before = jnp.where(col == 0, left, pltpu.roll(center, 1, 1))
    after = jnp.where(col == side - 1, right, pltpu.roll(center, side - 1, 1))
    return above, below, before, after


def image_kernel(
    rows, cols, order, tile, slot, first, last, sun,
    pixels, center, up, down, left, right, lit,
    obs_x, obs_y, fit_x, fit_y, cross, power,
    inv_s, px_s, py_s, ox_s, oy_s, fx_s, fy_s,
):
    i = pl.program_id(0)
    side = center.shape[1]

    @pl.when(i == 0)
    def start_sums():
        cross[...] = jnp.zeros_like(cross)
        power[...] = jnp.zeros_like(power)

    @pl.when(first[i] == 1)
    def start_tile():
        g_up, g_down, g_left, g_right = edges(tile[i], rows, cols)
        above, below, before, after = shifted(
            center[0],
            up[0, 7:8, :] * g_up,
            down[0, 0:1, :] * g_down,
            left[0, :, 127:128] * g_left,
            right[0, :, 0:1] * g_right,
        )
        slope_x = (after - before) * 0.5
        slope_y = (below - above) * 0.5
        inverse = lax.rsqrt(1.0 + slope_x * slope_x + slope_y * slope_y)
        inv_s[...] = inverse
        px_s[...] = slope_x * inverse
        py_s[...] = slope_y * inverse
        zero = jnp.zeros((side, side), jnp.float32)
        ox_s[...] = zero
        oy_s[...] = zero
        fx_s[...] = zero
        fy_s[...] = zero

    k = order[i]
    sx, sy, sz, gain = sun[4 * k], sun[4 * k + 1], sun[4 * k + 2], sun[4 * k + 3]
    scale = sharpness * LOG2E
    ux, uy, uz = sx * scale, sy * scale, sz * scale
    refl_scale = gain * (1.0 / (sharpness * LOG2E))
    gx, gy = gain * sx, gain * sy
    gc = gain * (1.0 / scale)

    def step(j, sums):
        at = pl.ds(pl.multiple_of(j * CHUNK, CHUNK), CHUNK)
        inverse, px, py = inv_s[at, :], px_s[at, :], py_s[at, :]
        observed = pixels[0, at, :].astype(jnp.float32)
        shine = lit[0, at, :].astype(jnp.float32)
        u = uz * inverse - ux * px - uy * py
        soft = jnp.log2(1.0 + jnp.exp2(u))
        sigma = 1.0 - jnp.exp2(-soft)
        q = soft * refl_scale
        v = u * gc
        dx = gx + v * px
        dy = gy + v * py
        seen = sigma * observed
        model = sigma * q
        ox_s[at, :] += seen * dx
        oy_s[at, :] += seen * dy
        fx_s[at, :] += model * dx
        fy_s[at, :] += model * dy
        shone = shine * q
        return sums[0] + shone * observed, sums[1] + shone * q

    zero = jnp.zeros((CHUNK, side), jnp.float32)
    sums = lax.fori_loop(0, side // CHUNK, step, (zero, zero), unroll=2)
    cross[...] += sums[0]
    power[...] += sums[1]

    @pl.when(last[i] == 1)
    def end_tile():
        factor = inv_s[...] * (-lit[0].astype(jnp.float32))
        obs_x[0] = (ox_s[...] * factor).astype(obs_x.dtype)
        obs_y[0] = (oy_s[...] * factor).astype(obs_y.dtype)
        fit_x[0] = (fx_s[...] * factor).astype(fit_x.dtype)
        fit_y[0] = (fy_s[...] * factor).astype(fit_y.dtype)


def image_sums(rows, cols, plan, sun, pixels, surface_all, lit_all):
    order, tile, slot, first, last = plan
    images, side = pixels.shape[0], pixels.shape[1]
    tiles = rows * cols
    slots = min(tiles, images)
    by_tile = lambda i, order, tile, *rest: tile[i]
    field = jax.ShapeDtypeStruct((slots, side, side), jnp.float32)
    part = jax.ShapeDtypeStruct((CHUNK, side), jnp.float32)
    field_spec = pl.BlockSpec((1, side, side), lambda i, order, tile, slot, *rest: (slot[i], 0, 0))
    part_spec = pl.BlockSpec((CHUNK, side), lambda i, *rest: (0, 0))
    return pl.pallas_call(
        functools.partial(image_kernel, rows, cols),
        out_shape=[field] * 4 + [part] * 2,
        grid_spec=pltpu.PrefetchScalarGridSpec(
            num_scalar_prefetch=6,
            grid=(images,),
            in_specs=[pl.BlockSpec((1, side, side), lambda i, order, *rest: (order[i], 0, 0))]
            + rim_specs(side, cols, tiles, by_tile)
            + [pl.BlockSpec((1, side, side), lambda i, order, tile, *rest: (tile[i], 0, 0))],
            out_specs=[field_spec] * 4 + [part_spec] * 2,
            scratch_shapes=[pltpu.VMEM((side, side), jnp.float32)] * 7,
        ),
        compiler_params=pltpu.CompilerParams(vmem_limit_bytes=40 * 2**20),
        name="image_sums",
    )(order, tile, slot, first, last, sun, pixels, *([surface_all] * 5), lit_all)


def data_kernel(
    rows, cols, slot, seen, albedo,
    ox, ox_l, ox_r, fx, fx_l, fx_r, oy, oy_u, oy_d, fy, fy_u, fy_d, out,
):
    t = pl.program_id(0)
    tiles = rows * cols
    g_up, g_down, g_left, g_right = edges(t, rows, cols)
    a = albedo[0]
    has = lambda n: jnp.where(seen[jnp.clip(n, 0, tiles - 1)] == 1, a, 0.0)
    here, above, below = has(t), has(t - cols) * g_up, has(t + cols) * g_down
    before, after = has(t - 1) * g_left, has(t + 1) * g_right
    mix = lambda f, o, gate: (a * f - o) * gate
    grad_x = mix(fx[0], ox[0], here)
    grad_y = mix(fy[0], oy[0], here)
    side = grad_x.shape[0]
    left = mix(fx_l[0, :, 127:128], ox_l[0, :, 127:128], before)
    right = mix(fx_r[0, :, 0:1], ox_r[0, :, 0:1], after)
    up = mix(fy_u[0, 7:8, :], oy_u[0, 7:8, :], above)
    down = mix(fy_d[0, 0:1, :], oy_d[0, 0:1, :], below)
    row = lax.broadcasted_iota(jnp.int32, grad_x.shape, 0)
    col = lax.broadcasted_iota(jnp.int32, grad_x.shape, 1)
    y_above = jnp.where(row == 0, up, pltpu.roll(grad_y, 1, 0))
    y_below = jnp.where(row == side - 1, down, pltpu.roll(grad_y, side - 1, 0))
    x_before = jnp.where(col == 0, left, pltpu.roll(grad_x, 1, 1))
    x_after = jnp.where(col == side - 1, right, pltpu.roll(grad_x, side - 1, 1))
    out[0] = ((x_before - x_after) * 0.5 + (y_above - y_below) * 0.5).astype(out.dtype)


def data_part(rows, cols, slot, seen, albedo, obs_x, obs_y, fit_x, fit_y):
    side = obs_x.shape[1]
    tiles = rows * cols
    center, up, down, left, right = rim_specs(side, cols, tiles, lambda t, *rest: t)

    def through(spec):
        def index(t, slot, *rest):
            place = spec.index_map(t)
            return (slot[place[0]],) + place[1:]

        return pl.BlockSpec(spec.block_shape, index)

    center, up, down, left, right = map(through, (center, up, down, left, right))
    return pl.pallas_call(
        functools.partial(data_kernel, rows, cols),
        out_shape=jax.ShapeDtypeStruct((tiles, side, side), jnp.float32),
        grid_spec=pltpu.PrefetchScalarGridSpec(
            num_scalar_prefetch=3,
            grid=(tiles,),
            in_specs=[center, left, right] * 2 + [center, up, down] * 2,
            out_specs=pl.BlockSpec((1, side, side), lambda t, *rest: (t, 0, 0)),
        ),
        compiler_params=pltpu.CompilerParams(vmem_limit_bytes=40 * 2**20),
        name="data_part",
    )(
        slot, seen, albedo,
        obs_x, obs_x, obs_x, fit_x, fit_x, fit_x, obs_y, obs_y, obs_y, fit_y, fit_y, fit_y,
    )


def update_kernel(rows, cols, me, center, up, down, left, right, data, out):
    g_up, g_down, g_left, g_right = edges(me[0], rows, cols)
    surface = center[0]
    above, below, before, after = shifted(
        surface,
        up[0, 7:8, :] * g_up,
        down[0, 0:1, :] * g_down,
        left[0, :, 127:128] * g_left,
        right[0, :, 0:1] * g_right,
    )
    laplace = below + above + after + before - 4.0 * surface
    out[...] = surface - step_size * (data[...].astype(jnp.float32) - smooth_weight * laplace)


def update(rows, cols, me, surface_all, data):
    side = data.shape[0]
    whole = pl.BlockSpec((side, side), lambda i, me: (0, 0))
    return pl.pallas_call(
        functools.partial(update_kernel, rows, cols),
        out_shape=jax.ShapeDtypeStruct((side, side), jnp.float32),
        grid_spec=pltpu.PrefetchScalarGridSpec(
            num_scalar_prefetch=1,
            grid=(1,),
            in_specs=rim_specs(side, cols, rows * cols, lambda i, me: me[0]) + [whole],
            out_specs=whole,
        ),
        compiler_params=pltpu.CompilerParams(vmem_limit_bytes=40 * 2**20),
        name="update",
    )(me, *([surface_all] * 5), data)


def total_kernel(rows, cols, part, total, held, send_sem, recv_sem):
    devices = rows * cols
    me = lax.axis_index("row") * cols + lax.axis_index("col")
    barrier = pltpu.get_barrier_semaphore()

    def place(step):
        peer = lax.rem(me + step, devices)
        return peer, (peer // cols, lax.rem(peer, cols))

    def greet(step, carry):
        unused, device = place(step)
        pl.semaphore_signal(barrier, inc=1, device_id=device, device_id_type=pl.DeviceIdType.MESH)
        return carry

    lax.fori_loop(1, devices, greet, 0)
    pl.semaphore_wait(barrier, devices - 1)

    def copy(step):
        unused, device = place(step)
        return pltpu.make_async_remote_copy(
            src_ref=part,
            dst_ref=held.at[step],
            send_sem=send_sem.at[step],
            recv_sem=recv_sem.at[step],
            device_id=device,
            device_id_type=pl.DeviceIdType.MESH,
        )

    def send(step, carry):
        copy(step).start()
        return carry

    def land(step, carry):
        copy(step).wait()
        return carry

    held[0] = part[...]
    lax.fori_loop(1, devices, send, 0)
    lax.fori_loop(1, devices, land, 0)
    total[...] = jnp.sum(held[...], axis=0)


def total_over_devices(rows, cols, part):
    devices = rows * cols
    return pl.pallas_call(
        functools.partial(total_kernel, rows, cols),
        out_shape=jax.ShapeDtypeStruct(part.shape, jnp.float32),
        in_specs=[pl.BlockSpec(memory_space=pltpu.VMEM)],
        out_specs=pl.BlockSpec(memory_space=pltpu.VMEM),
        scratch_shapes=[
            pltpu.VMEM((devices,) + part.shape, jnp.float32),
            pltpu.SemaphoreType.DMA((devices,)),
            pltpu.SemaphoreType.DMA((devices,)),
        ],
        compiler_params=pltpu.CompilerParams(collective_id=0, has_side_effects=True),
        name="total",
    )(part)


def image_plan(dest, tiles):
    count = dest.shape[0]
    place = jnp.arange(count)
    earlier = (dest[None, :] < dest[:, None]) | (
        (dest[None, :] == dest[:, None]) & (place[None, :] < place[:, None])
    )
    rank = jnp.sum(earlier, axis=1)
    chosen = rank[None, :] == place[:, None]
    order = jnp.sum(jnp.where(chosen, place[None, :], 0), axis=1).astype(jnp.int32)
    tile = jnp.sum(jnp.where(chosen, dest[None, :], 0), axis=1).astype(jnp.int32)
    seen = jnp.any(dest[None, :] == jnp.arange(tiles)[:, None], axis=1)
    before = jnp.arange(tiles)[None, :] < jnp.arange(tiles)[:, None]
    tile_slot = jnp.where(seen, jnp.sum(before & seen[None, :], axis=1), 0).astype(jnp.int32)
    slot = jnp.sum(
        jnp.where(tile[:, None] == jnp.arange(tiles)[None, :], tile_slot[None, :], 0), axis=1
    ).astype(jnp.int32)
    change = (tile[1:] != tile[:-1]).astype(jnp.int32)
    one = jnp.ones((1,), jnp.int32)
    first = jnp.concatenate([one, change])
    last = jnp.concatenate([change, one])
    return (order, tile, slot, first, last), tile_slot, seen.astype(jnp.int32)


def body(heights, shadow, image_tiles, image_dest, sun_gain, shot_dest, shot_pixel, shot_height):
    rows, cols = lax.axis_size("row"), lax.axis_size("col")
    tiles = rows * cols
    side = heights.shape[0]
    me = (lax.axis_index("row") * cols + lax.axis_index("col")).astype(jnp.int32).reshape(1)
    plan, tile_slot, seen = image_plan(image_dest[:, 0], tiles)
    sun = sun_gain.astype(jnp.float32).reshape(-1)
    lit_all = lax.all_gather((1.0 - shadow.astype(jnp.float32)).astype(jnp.bfloat16), AXES)
    shot_at = (shot_dest[:, 0], shot_pixel // side, lax.rem(shot_pixel, side))
    surface = heights
    for sweep in range(ITERS):
        surface_all = lax.all_gather(surface, AXES)
        obs_x, obs_y, fit_x, fit_y, cross, power = image_sums(
            rows, cols, plan, sun, image_tiles, surface_all, lit_all
        )
        sums = jnp.stack([jnp.sum(cross), jnp.sum(power)])
        sums = jnp.broadcast_to(sums[:, None, None], (2, 4, 128)).reshape(8, 128)
        sums = total_over_devices(rows, cols, sums)
        albedo = (sums[0, 0] / sums[4, 0]).reshape(1)
        data = data_part(rows, cols, tile_slot, seen, albedo, obs_x, obs_y, fit_x, fit_y)
        misfit = laser_weight * (surface_all[shot_at] - shot_height)
        data = data.at[shot_at].add(misfit)
        data = lax.psum_scatter(data.astype(LINK), AXES, scatter_dimension=0, tiled=False)
        surface = update(rows, cols, me, surface_all, data)
    return surface


def solution(mesh):
    placed = (
        P("row", "col"),
        P("row", "col"),
        P(("row", "col"), None, None),
        P(("row", "col"), None),
        P(("row", "col"), None),
        P(("row", "col"), None),
        P(("row", "col")),
        P(("row", "col")),
    )
    return jax.shard_map(
        body, mesh=mesh, in_specs=placed, out_specs=P("row", "col"), check_vma=False
    )
```

time: 748 us -> 937 us (1.25)
  Pallas kernels: 0 us -> 216 us
  waiting for transfers between devices: 384 us -> 583 us
  other arithmetic: 184 us -> 78.1 us
  blocking collectives: 81.8 us -> 0 us
  starting transfers between devices: 53.8 us -> 0.17 us
  between operations: 3.36 us -> 16 us
    reduce_scatter x0 -> x2, waiting for transfers between devices: none -> 366 us  [body(): lax.psum_scatter(data.astype(LINK), AXES, scatter_dimension=0, tiled=False)]
    all_to_all x4 -> x0, waiting for transfers between devices: 284 us -> none  [the longest x1 281 us: body(): lax.all_to_all(send_pixels, ('row', 'col'), split_axis=0, concat_axis=0,...]
    all_gather x0 -> x3, waiting for transfers between devices: none -> 217 us  [the longest x2 156 us: body(): surface_all = lax.all_gather(surface, AXES)]
    pallas_call x0 -> x8, Pallas kernels: none -> 216 us  [the longest x2 130 us: image_sums(): pl.pallas_call(functools.partial(image_kernel, rows, cols), out_shape=[fi...]
    reduce_sum x12 -> x8, other arithmetic: 154 us -> 4.33 us  [the longest x4 2.43 us: body(): sums = jnp.stack([jnp.sum(cross), jnp.sum(power)])]
    ppermute x16 -> x0, waiting for transfers between devices: 100 us -> none  [the longest x8 83.7 us: with_halo(): after = lax.ppermute(initial, axis, down)]
    psum x2 -> x0, blocking collectives: 81.8 us -> none  [body(): lax.psum((jnp.sum(lit * cross), jnp.sum(lit * power)), ('row', 'col'))]
    scatter-add x2, other arithmetic: 6.76 us -> 67.2 us  [body(): data = data.at[shot_at].add(misfit)]
  transfers between devices with their start and end apart: 20 -> 5, of which waited for: 12 -> 5; matrix products, arithmetic and copies ran while one was open for 17% -> 1% of each run, Pallas kernels for 0% -> 0%
where the time goes in v1:
time: 937 us; the launch traced here: 932 us
  waiting for transfers between devices  583 us (62%)
  Pallas kernels  216 us (23%)
  other arithmetic  78.1 us (8%)
  local copies, waits for them, and re-layouts  38.3 us (4%)
  between operations  16 us (2%)
    reduce_scatter x2, waiting for transfers between devices, body(): lax.psum_scatter(data.astype(LINK), AXES, scatter_dimension=0, tiled=False)  366 us
    all_gather x2, waiting for transfers between devices, body(): surface_all = lax.all_gather(surface, AXES)  156 us
    pallas_call x2, Pallas kernels, image_sums(): pl.pallas_call(functools.partial(image_kernel, rows, cols), out_shape=[fi...  130 us
    scatter-add x2, other arithmetic, body(): data = data.at[shot_at].add(misfit)  67.2 us
    pallas_call x2, Pallas kernels, data_part(): pl.pallas_call(functools.partial(data_kernel, rows, cols), out_shape=jax....  62.4 us
    all_gather x1, waiting for transfers between devices, body(): lax.all_gather((1.0 - shadow.astype(jnp.float32)).astype(jnp.bfloat16), A...  61.1 us
    unnamed x22, local copies, waits for them, and re-layouts  25.8 us
    pallas_call x2, Pallas kernels, total_over_devices(): pl.pallas_call(functools.partial(total_kernel, rows, cols), out_shape=jax...  21.9 us
  transfers between devices with their start and end apart: 5, of which 5 were waited for; matrix products, arithmetic and copies ran while one was open for 1% of the time, Pallas kernels for 0%

profile of v1, /device:TPU:0, one launch (start us, length us, event | category | flops | bytes accessed | tf_op | source)
XLA Modules:
  0.0 931.6 jit_solution(2258539522564285117)
XLA Ops:
  6.5 0.0 all-gather.9.cloned.1.call-start
  6.5 1.6 subtract_convert_fusion
  8.2 0.0 all-gather.9.cloned.1.call-update
  8.2 0.0 all-gather.7.cloned.1.call-start
  8.2 0.7 all-gather.7.cloned.1.call-update
  8.9 0.0 reduce-scatter.3.cloned.1.call-start
  9.0 0.8 copy.10
  9.8 0.1 reshape.39.sun
  9.9 0.8 fusion.2
  10.7 0.9 convert_reduce_fusion
  11.6 0.8 select_reduce_fusion
  12.3 0.1 compare_convert_fusion
  12.4 0.1 pad_add_fusion.1
  12.5 0.1 convert_reduce_fusion.1
  12.6 0.1 select_reduce_fusion.2.slot
  12.7 0.7 compare_select_fusion.2
  13.4 0.7 or_select_fusion
  14.1 61.1 %all-gather.9.cloned.1.call-done = bf16[8192,256]{1,0:T(8,128)(2,1)} async-done(((bf16[256,256]{1,0:T(8,128)(2,1)}), bf16[8192,256]{1,0:T(8,128)(2,1)}) %all-gather.9.cloned.1.call-update) | async-done | bytes 4194320 | tf_op jit(solution)/shard_map/all_gather | solution.py:342
  75.2 78.8 %all-gather.7.cloned.1.call-done = f32[8192,256]{1,0:T(8,128)} async-done(((f32[256,256]{1,0:T(8,128)}), f32[8192,256]{1,0:T(8,128)}) %all-gather.7.cloned.1.call-update) | async-done | bytes 8388624 | tf_op jit(solution)/shard_map/all_gather | solution.py:346
  154.1 2.2 copy-done.6
  156.3 64.8 %image_sums.2 = (f32[32,256,256]{2,1,0:T(8,128)S(1)}, f32[32,256,256]{2,1,0:T(8,128)}, f32[32,256,256]{2,1,0:T(8,128)}, f32[32,256,256]{2,1,0:T(8,128)}, f32[16,256]{1,0:T(8,128)S(1)}, /*index=5*/f32[16,256]{1,0:T(8,128)S(1)}) custom-call(s32[64]{0:T(128)S(1)} %get-tuple-element.30.order, s32[64]{0:T(128)S(1)} %get-tuple-element.29.tile, ...), custom_call_target="tpu_custom_call" | custom-call | tf_op jit(solution)/shard_map/image_sums/pallas_call | solution.py:147
  221.1 3.2 copy-done.3
  224.3 0.7 reduce_sum.86
  224.9 0.6 reduce_sum.87
  225.5 1.3 pad_maximum_fusion
  226.9 0.1 broadcast_in_dim.82
  226.9 0.1 broadcast_in_dim.83
  227.0 0.7 broadcast_in_dim.84.part
  227.7 10.9 %total.2 = f32[8,128]{1,0:T(8,128)} custom-call(f32[8,128]{1,0:T(8,128)} %broadcast_in_dim.84.part), custom_call_target="tpu_custom_call" | custom-call | tf_op jit(solution)/shard_map/total/pallas_call | solution.py:297
  238.6 1.3 fusion.8
  239.9 3.7 gather_fusion
  245.0 31.2 %data_part.2 = f32[32,256,256]{2,1,0:T(8,128)S(1)} custom-call(s32[32]{0:T(128)S(1)} %broadcast_select_fusion.slot, s32[32]{0:T(128)S(1)} %convert_element_type.20.seen, f32[1]{0:T(128)} %bitcast.6.albedo, f32[32,256,256]{2,1,0:T(8,128)} %copy-done.3, f32[32,256,256]{2,1,0:T(8,128)} %copy-done.3, f32[32,256,256]{2,1,0:T(8,128)} %copy-done.3, ...), custom_call_target="tpu_custom_call" | custom-call | tf_op jit(solution)/shard_map/data_part/pallas_call | solution.py:205
  276.2 3.2 copy-done.5
  279.4 33.6 %scatter_fusion = f32[32,256,256]{2,1,0:T(8,128)} fusion(f32[32,256,256]{2,1,0:T(8,128)} %copy-done.5, s32[256]{0:T(256)S(1)} %bitcast.43, f32[256]{0:T(256)S(1)} %subtract_multiply_fusion.1), kind=kCustom, calls=%fused_computation.2 | custom fusion | flops 256 | bytes 6144 | tf_op jit(solution)/shard_map/scatter-add | solution.py:356
  313.0 0.0 reduce-scatter.3.cloned.1.call-update
  313.0 0.0 all-gather.11.cloned.1.call-start
  313.0 182.9 %reduce-scatter.3.cloned.1.call-done = f32[1,256,256]{2,1,0:T(8,128)} async-done(((f32[32,256,256]{2,1,0:T(8,128)}), f32[1,256,256]{2,1,0:T(8,128)}) %reduce-scatter.3.cloned.1.call-update) | async-done | bytes 262160 | tf_op jit(solution)/shard_map/reduce_scatter | solution.py:357
  496.0 3.4 copy-done
  499.3 0.9 copy-done.8
  500.3 1.0 update.2
  501.3 0.0 all-gather.11.cloned.1.call-update
  501.3 0.0 reduce-scatter.5.cloned.1.call-start
  501.4 77.0 %all-gather.11.cloned.1.call-done = f32[8192,256]{1,0:T(8,128)} async-done(((f32[256,256]{1,0:T(8,128)}), f32[8192,256]{1,0:T(8,128)}) %all-gather.11.cloned.1.call-update) | async-done | bytes 8388624 | tf_op jit(solution)/shard_map/all_gather | solution.py:346
  578.3 2.2 copy-done.7
  580.5 64.8 %image_sums.3 = (f32[32,256,256]{2,1,0:T(8,128)S(1)}, f32[32,256,256]{2,1,0:T(8,128)}, f32[32,256,256]{2,1,0:T(8,128)}, f32[32,256,256]{2,1,0:T(8,128)}, f32[16,256]{1,0:T(8,128)S(1)}, /*index=5*/f32[16,256]{1,0:T(8,128)S(1)}) custom-call(s32[64]{0:T(128)S(1)} %get-tuple-element.30.order, s32[64]{0:T(128)S(1)} %get-tuple-element.29.tile, ...), custom_call_target="tpu_custom_call" | custom-call | tf_op jit(solution)/shard_map/image_sums/pallas_call | solution.py:147
  645.3 3.2 copy-done.2
  648.5 3.7 gather_fusion.1
  652.2 0.6 reduce_sum.88
  652.8 0.6 reduce_sum.89
  653.4 1.3 pad_maximum_fusion.1
  654.7 0.1 broadcast_in_dim.87
  654.7 0.1 broadcast_in_dim.88
  654.8 0.7 broadcast_in_dim.89.part
  655.5 10.9 %total.3 = f32[8,128]{1,0:T(8,128)} custom-call(f32[8,128]{1,0:T(8,128)} %broadcast_in_dim.89.part), custom_call_target="tpu_custom_call" | custom-call | tf_op jit(solution)/shard_map/total/pallas_call | solution.py:297
  666.4 1.3 fusion.7
  669.1 31.2 %data_part.3 = f32[32,256,256]{2,1,0:T(8,128)S(1)} custom-call(s32[32]{0:T(128)S(1)} %broadcast_select_fusion.slot, s32[32]{0:T(128)S(1)} %convert_element_type.20.seen, f32[1]{0:T(128)} %bitcast.15.albedo, f32[32,256,256]{2,1,0:T(8,128)} %copy-done.2, f32[32,256,256]{2,1,0:T(8,128)} %copy-done.2, f32[32,256,256]{2,1,0:T(8,128)} %copy-done.2, ...), custom_call_target="tpu_custom_call" | custom-call | tf_op jit(solution)/shard_map/data_part/pallas_call | solution.py:205
  700.3 0.0 copy-start.4
  700.3 3.2 copy-done.4
  703.5 33.6 %scatter_fusion.1 = f32[32,256,256]{2,1,0:T(8,128)} fusion(f32[32,256,256]{2,1,0:T(8,128)} %copy-done.4, s32[256]{0:T(256)S(1)} %bitcast.44, f32[256]{0:T(256)S(1)} %subtract_multiply_fusion), kind=kCustom, calls=%fused_computation.3 | custom fusion | flops 256 | bytes 6144 | tf_op jit(solution)/shard_map/scatter-add | solution.py:356
  737.1 0.0 reduce-scatter.5.cloned.1.call-update
  737.1 182.6 %reduce-scatter.5.cloned.1.call-done = f32[1,256,256]{2,1,0:T(8,128)} async-done(((f32[32,256,256]{2,1,0:T(8,128)}), f32[1,256,256]{2,1,0:T(8,128)}) %reduce-scatter.5.cloned.1.call-update) | async-done | bytes 262160 | tf_op jit(solution)/shard_map/reduce_scatter | solution.py:357
  919.7 3.4 copy-done.1
  923.1 0.9 copy-done.9
  924.0 1.0 update.3
  (15 shorter events, 0.0 us)
Async XLA Ops:
  6.5 68.7 %all-gather.9.cloned.1.call-start = ((), (), s32[]{:S(2)}) async-start(), calls=%async_computation.5 | async-start | bytes 4325376 | tf_op jit(solution)/shard_map/all_gather | solution.py:342
  8.2 145.9 %all-gather.7.cloned.1.call-start = ((), (), s32[]{:S(2)}) async-start(), calls=%async_computation.4 | async-start | bytes 8650752 | tf_op jit(solution)/shard_map/all_gather | solution.py:346
  8.9 487.0 %reduce-scatter.3.cloned.1.call-start = ((), (), s32[]{:S(2)}) async-start(), calls=%async_computation.2 | async-start | bytes 8650752 | tf_op jit(solution)/shard_map/reduce_scatter | solution.py:357
  154.1 2.2 copy-start.6
  156.3 88.7 %copy-start.10 = (f32[256]{0:T(256)S(1)}, f32[256]{0:T(256)}, u32[]{:S(2)}) copy-start(f32[256]{0:T(256)} %param.15) | copy-start | bytes 3076
  221.1 3.2 copy-start.3
  276.1 3.2 copy-start.5
  313.0 265.4 %all-gather.11.cloned.1.call-start = ((), (), s32[]{:S(2)}) async-start(), calls=%async_computation.6 | async-start | bytes 8650752 | tf_op jit(solution)/shard_map/all_gather | solution.py:346
  496.0 3.4 copy-start
  499.3 0.9 copy-start.8
  501.3 418.4 %reduce-scatter.5.cloned.1.call-start = ((), (), s32[]{:S(2)}) async-start(), calls=%async_computation.3 | async-start | bytes 8650752 | tf_op jit(solution)/shard_map/reduce_scatter | solution.py:357
  578.3 2.2 copy-start.7
  645.3 3.2 copy-start.2
  700.3 3.2 copy-start.4
  919.7 3.4 copy-start.1
  923.1 0.9 copy-start.9
Sparse Core Ops, SparseCore 0:
  10.4 64.7 all-gather.8
  78.2 75.8 all-gather.6
  313.1 182.8 reduce-scatter.2
  501.4 76.8 all-gather.10
  737.2 182.4 reduce-scatter.4

commit v2 on v1

--- a/solution.py
+++ b/solution.py
@@ -18,7 +18,7 @@
 AXES = ("row", "col")
 LOG2E = math.log2(math.e)
 CHUNK = 16
-LINK = jnp.float32
+LINK = jnp.bfloat16
 
 
 def rim_specs(side, cols, tiles, tile_of):
@@ -162,8 +162,8 @@
 
 
 def data_kernel(
-    rows, cols, slot, seen, albedo,
-    ox, ox_l, ox_r, fx, fx_l, fx_r, oy, oy_u, oy_d, fy, fy_u, fy_d, out,
+    rows, cols, slot, seen, albedo, shot_start, shot_pixel, shot_height,
+    ox, ox_l, ox_r, fx, fx_l, fx_r, oy, oy_u, oy_d, fy, fy_u, fy_d, surface, out,
 ):
     t = pl.program_id(0)
     tiles = rows * cols
@@ -186,10 +186,20 @@
     y_below = jnp.where(row == side - 1, down, pltpu.roll(grad_y, side - 1, 0))
     x_before = jnp.where(col == 0, left, pltpu.roll(grad_x, 1, 1))
     x_after = jnp.where(col == side - 1, right, pltpu.roll(grad_x, side - 1, 1))
-    out[0] = ((x_before - x_after) * 0.5 + (y_above - y_below) * 0.5).astype(out.dtype)
-
-
-def data_part(rows, cols, slot, seen, albedo, obs_x, obs_y, fit_x, fit_y):
+    out[0] = (x_before - x_after) * 0.5 + (y_above - y_below) * 0.5
+    lane = lax.broadcasted_iota(jnp.int32, (1, side), 1)
+
+    def shot(n, carry):
+        pixel = shot_pixel[n]
+        at = pl.ds(pixel // side, 1)
+        misfit = laser_weight * (surface[0, at, :] - shot_height[n])
+        out[0, at, :] += jnp.where(lane == lax.rem(pixel, side), misfit, 0.0)
+        return carry
+
+    lax.fori_loop(shot_start[t], shot_start[t + 1], shot, 0)
+
+
+def data_part(rows, cols, slot, seen, albedo, shots, surface_all, obs_x, obs_y, fit_x, fit_y):
     side = obs_x.shape[1]
     tiles = rows * cols
     center, up, down, left, right = rim_specs(side, cols, tiles, lambda t, *rest: t)
@@ -206,16 +216,19 @@
         functools.partial(data_kernel, rows, cols),
         out_shape=jax.ShapeDtypeStruct((tiles, side, side), jnp.float32),
         grid_spec=pltpu.PrefetchScalarGridSpec(
-            num_scalar_prefetch=3,
+            num_scalar_prefetch=6,
             grid=(tiles,),
-            in_specs=[center, left, right] * 2 + [center, up, down] * 2,
+            in_specs=[center, left, right] * 2
+            + [center, up, down] * 2
+            + [pl.BlockSpec((1, side, side), lambda t, *rest: (t, 0, 0))],
             out_specs=pl.BlockSpec((1, side, side), lambda t, *rest: (t, 0, 0)),
         ),
         compiler_params=pltpu.CompilerParams(vmem_limit_bytes=40 * 2**20),
         name="data_part",
     )(
-        slot, seen, albedo,
+        slot, seen, albedo, *shots,
         obs_x, obs_x, obs_x, fit_x, fit_x, fit_x, obs_y, obs_y, obs_y, fit_y, fit_y, fit_y,
+        surface_all,
     )
 
 
@@ -307,6 +320,163 @@
         compiler_params=pltpu.CompilerParams(collective_id=0, has_side_effects=True),
         name="total",
     )(part)
+
+
+def add_kernel(
+    rows, cols, data, out,
+    own, got1, send2, got2, send3, got3, send4, got4,
+    load_sem, ss1, rs1, ss2, rs2, ss3, rs3, ss4, rs4,
+):
+    X, Z = rows // 2, cols // 2
+    side = out.shape[0]
+    r, c = lax.axis_index("row"), lax.axis_index("col")
+    x, k, z, y = r // 2, lax.rem(r, 2), c // 2, lax.rem(c, 2)
+    core_peer = (x * 2 + 1 - k, c)
+    y_peer = (r, z * 2 + 1 - y)
+    x_at = [lax.rem(x + d, X) for d in range(X)]
+    z_at = [lax.rem(z + e + 1, Z) for e in range(Z)]
+    x_peers = [None] + [(x_at[d] * 2 + k, c) for d in range(1, X)]
+    z_peers = [(r, z_at[e] * 2 + y) for e in range(Z - 1)]
+
+    barrier = pltpu.get_barrier_semaphore()
+    peers = [core_peer, y_peer] + x_peers[1:] + z_peers
+    for peer in peers:
+        pl.semaphore_signal(barrier, inc=1, device_id=peer, device_id_type=pl.DeviceIdType.MESH)
+    pl.semaphore_wait(barrier, len(peers))
+
+    def remote(src, dst, send, recv, peer):
+        return pltpu.make_async_remote_copy(
+            src_ref=src, dst_ref=dst, send_sem=send, recv_sem=recv,
+            device_id=peer, device_id_type=pl.DeviceIdType.MESH,
+        )
+
+    first = [
+        remote(data.at[:, 1 - k, z_at[e]], got1.at[e], ss1.at[e], rs1.at[e], core_peer)
+        for e in range(Z)
+    ]
+    loads = [
+        pltpu.make_async_copy(data.at[:, k, z_at[e]], own.at[e], load_sem.at[e]) for e in range(Z)
+    ]
+    second = [
+        [
+            remote(send2.at[e, d - 1], got2.at[e, d - 1], ss2.at[e, d - 1], rs2.at[e, d - 1], x_peers[d])
+            for d in range(1, X)
+        ]
+        for e in range(Z)
+    ]
+    third = [remote(send3.at[e], got3.at[e], ss3.at[e], rs3.at[e], y_peer) for e in range(Z)]
+    fourth = [
+        remote(send4.at[e], got4.at[e], ss4.at[e], rs4.at[e], z_peers[e]) for e in range(Z - 1)
+    ]
+    for e in range(Z):
+        first[e].start()
+        loads[e].start()
+
+    def by_rows(work):
+        def step(j, carry):
+            work(pl.ds(pl.multiple_of(j * 32, 32), 32))
+            return carry
+
+        lax.fori_loop(0, side // 32, step, 0)
+
+    def over_x(e, which, at):
+        total = own[e, x, which, at, :] + got1[e, x, which, at, :]
+        for d in range(1, X):
+            total = total + got2[e, d - 1, which, at, :].astype(jnp.float32)
+        return total
+
+    def stage2(e):
+        loads[e].wait()
+        first[e].wait_recv()
+        for d in range(1, X):
+
+            def work(at):
+                for which in range(2):
+                    total = own[e, x_at[d], which, at, :] + got1[e, x_at[d], which, at, :]
+                    send2[e, d - 1, which, at, :] = total.astype(LINK)
+
+            by_rows(work)
+            second[e][d - 1].start()
+
+    def stage3(e):
+        for copy in second[e]:
+            copy.wait_recv()
+
+        def work(at):
+            send3[e, at, :] = over_x(e, 1 - y, at).astype(LINK)
+
+        by_rows(work)
+        third[e].start()
+
+    def stage4(e):
+        third[e].wait_recv()
+
+        def work(at):
+            total = over_x(e, y, at) + got3[e, at, :].astype(jnp.float32)
+            if e < Z - 1:
+                send4[e, at, :] = total.astype(LINK)
+            else:
+                out[at, :] = total
+
+        by_rows(work)
+        if e < Z - 1:
+            fourth[e].start()
+
+    for t in range(Z + 2):
+        if t < Z:
+            stage2(t)
+        if 0 <= t - 1 < Z:
+            stage3(t - 1)
+        if 0 <= t - 2 < Z:
+            stage4(t - 2)
+    for copy in fourth:
+        copy.wait_recv()
+
+    def finish(at):
+        total = out[at, :]
+        for e in range(Z - 1):
+            total = total + got4[e, at, :].astype(jnp.float32)
+        out[at, :] = total
+
+    by_rows(finish)
+    for copy in first + [one for some in second for one in some] + third + fourth:
+        copy.wait_send()
+
+
+def add_parts(rows, cols, data):
+    X, Z = rows // 2, cols // 2
+    side = data.shape[-1]
+    vmem = lambda shape, dtype: pltpu.VMEM(shape + (side, side), dtype)
+    dma = pltpu.SemaphoreType.DMA
+    return pl.pallas_call(
+        functools.partial(add_kernel, rows, cols),
+        out_shape=jax.ShapeDtypeStruct((side, side), jnp.float32),
+        in_specs=[pl.BlockSpec(memory_space=pl.ANY)],
+        out_specs=pl.BlockSpec(memory_space=pltpu.VMEM),
+        scratch_shapes=[
+            vmem((Z, X, 2), jnp.float32),
+            vmem((Z, X, 2), jnp.float32),
+            vmem((Z, X - 1, 2), LINK),
+            vmem((Z, X - 1, 2), LINK),
+            vmem((Z,), LINK),
+            vmem((Z,), LINK),
+            vmem((Z - 1,), LINK),
+            vmem((Z - 1,), LINK),
+            dma((Z,)),
+            dma((Z,)),
+            dma((Z,)),
+            dma((Z, X - 1)),
+            dma((Z, X - 1)),
+            dma((Z,)),
+            dma((Z,)),
+            dma((Z - 1,)),
+            dma((Z - 1,)),
+        ],
+        compiler_params=pltpu.CompilerParams(
+            collective_id=1, has_side_effects=True, vmem_limit_bytes=56 * 2**20
+        ),
+        name="add_parts",
+    )(data.reshape(X, 2, Z, 2, side, side))
 
 
 def image_plan(dest, tiles):
@@ -332,6 +502,19 @@
     return (order, tile, slot, first, last), tile_slot, seen.astype(jnp.int32)
 
 
+def shot_plan(dest, pixel, height, tiles):
+    place = jnp.arange(dest.shape[0])
+    earlier = (dest[None, :] < dest[:, None]) | (
+        (dest[None, :] == dest[:, None]) & (place[None, :] < place[:, None])
+    )
+    rank = jnp.sum(earlier, axis=1)
+    chosen = rank[None, :] == place[:, None]
+    pixel = jnp.sum(jnp.where(chosen, pixel[None, :], 0), axis=1).astype(jnp.int32)
+    height = jnp.sum(jnp.where(chosen, height[None, :], 0.0), axis=1)
+    start = jnp.sum(dest[None, :] < jnp.arange(tiles + 1)[:, None], axis=1).astype(jnp.int32)
+    return start, pixel, height
+
+
 def body(heights, shadow, image_tiles, image_dest, sun_gain, shot_dest, shot_pixel, shot_height):
     rows, cols = lax.axis_size("row"), lax.axis_size("col")
     tiles = rows * cols
@@ -340,7 +523,7 @@
     plan, tile_slot, seen = image_plan(image_dest[:, 0], tiles)
     sun = sun_gain.astype(jnp.float32).reshape(-1)
     lit_all = lax.all_gather((1.0 - shadow.astype(jnp.float32)).astype(jnp.bfloat16), AXES)
-    shot_at = (shot_dest[:, 0], shot_pixel // side, lax.rem(shot_pixel, side))
+    shots = shot_plan(shot_dest[:, 0], shot_pixel, shot_height, tiles)
     surface = heights
     for sweep in range(ITERS):
         surface_all = lax.all_gather(surface, AXES)
@@ -351,10 +534,10 @@
         sums = jnp.broadcast_to(sums[:, None, None], (2, 4, 128)).reshape(8, 128)
         sums = total_over_devices(rows, cols, sums)
         albedo = (sums[0, 0] / sums[4, 0]).reshape(1)
-        data = data_part(rows, cols, tile_slot, seen, albedo, obs_x, obs_y, fit_x, fit_y)
-        misfit = laser_weight * (surface_all[shot_at] - shot_height)
-        data = data.at[shot_at].add(misfit)
-        data = lax.psum_scatter(data.astype(LINK), AXES, scatter_dimension=0, tiled=False)
+        data = data_part(
+            rows, cols, tile_slot, seen, albedo, shots, surface_all, obs_x, obs_y, fit_x, fit_y
+        )
+        data = add_parts(rows, cols, data)
         surface = update(rows, cols, me, surface_all, data)
     return surface
 

time: 937 us -> 574 us (0.61)
  waiting for transfers between devices: 583 us -> 216 us
  Pallas kernels: 216 us -> 295 us
  other arithmetic: 78.1 us -> 12.8 us
    reduce_scatter x2 -> x0, waiting for transfers between devices: 366 us -> none  [body(): lax.psum_scatter(data.astype(LINK), AXES, scatter_dimension=0, tiled=False)]
    pallas_call x0 -> x2, Pallas kernels: none -> 70.5 us  [add_parts(): pl.pallas_call(functools.partial(add_kernel, rows, cols), out_shape=jax.S...]
    scatter-add x2 -> x0, other arithmetic: 67.2 us -> none  [body(): data = data.at[shot_at].add(misfit)]
    unnamed x22 -> x20, local copies, waits for them, and re-layouts: 25.8 us -> 25.8 us
  transfers between devices with their start and end apart: 5 -> 3, of which waited for: 5 -> 3; matrix products, arithmetic and copies ran while one was open for 1% -> 1% of each run, Pallas kernels for 0% -> 0%
where the time goes in v2:
time: 574 us; the launch traced here: 570 us
  Pallas kernels  295 us (51%)
  waiting for transfers between devices  216 us (38%)
  local copies, waits for them, and re-layouts  31 us (5%)
  between operations  15.8 us (3%)
  other arithmetic  12.8 us (2%)
    all_gather x2, waiting for transfers between devices, body(): surface_all = lax.all_gather(surface, AXES)  156 us
    pallas_call x2, Pallas kernels, image_sums(): pl.pallas_call(functools.partial(image_kernel, rows, cols), out_shape=[fi...  130 us
    pallas_call x2, Pallas kernels, add_parts(): pl.pallas_call(functools.partial(add_kernel, rows, cols), out_shape=jax.S...  70.5 us
    pallas_call x2, Pallas kernels, data_part(): pl.pallas_call(functools.partial(data_kernel, rows, cols), out_shape=jax....  70.5 us
    all_gather x1, waiting for transfers between devices, body(): lax.all_gather((1.0 - shadow.astype(jnp.float32)).astype(jnp.bfloat16), A...  59.2 us
    unnamed x20, local copies, waits for them, and re-layouts  25.8 us
    pallas_call x2, Pallas kernels, total_over_devices(): pl.pallas_call(functools.partial(total_kernel, rows, cols), out_shape=jax...  21.6 us
  transfers between devices with their start and end apart: 3, of which 3 were waited for; matrix products, arithmetic and copies ran while one was open for 1% of the time, Pallas kernels for 0%

profile of v2, /device:TPU:0, one launch (start us, length us, event | category | flops | bytes accessed | tf_op | source)
XLA Modules:
  0.0 570.2 jit_solution(7223032874752012034)
XLA Ops:
  6.5 0.0 all-gather.9.cloned.1.call-start
  6.5 1.6 subtract_convert_fusion
  8.2 0.0 all-gather.9.cloned.1.call-update
  8.2 0.0 all-gather.7.cloned.1.call-start
  8.2 0.7 all-gather.7.cloned.1.call-update
  8.9 0.0 all-gather.11.cloned.1.call-start
  9.0 0.8 copy.10
  9.8 0.1 reshape.51.sun
  9.9 0.8 fusion.4
  10.7 0.9 convert_reduce_fusion.2
  11.6 0.8 select_reduce_fusion.2
  12.4 0.1 compare_convert_fusion
  12.4 0.1 pad_add_fusion.1
  12.5 0.1 convert_reduce_fusion.3
  12.6 0.8 convert_reduce_fusion.1.shot_start
  13.4 0.1 select_reduce_fusion.4.slot
  13.5 0.9 convert_reduce_fusion
  14.5 0.8 select_reduce_fusion.shot_height
  15.3 0.8 select_reduce_fusion.1.shot_pixel
  16.1 59.2 %all-gather.9.cloned.1.call-done = bf16[8192,256]{1,0:T(8,128)(2,1)} async-done(((bf16[256,256]{1,0:T(8,128)(2,1)}), bf16[8192,256]{1,0:T(8,128)(2,1)}) %all-gather.9.cloned.1.call-update) | async-done | bytes 4194320 | tf_op jit(solution)/shard_map/all_gather | solution.py:525
  75.2 78.8 %all-gather.7.cloned.1.call-done = f32[8192,256]{1,0:T(8,128)} async-done(((f32[256,256]{1,0:T(8,128)}), f32[8192,256]{1,0:T(8,128)}) %all-gather.7.cloned.1.call-update) | async-done | bytes 8388624 | tf_op jit(solution)/shard_map/all_gather | solution.py:529
  154.1 0.0 copy-start.6
  154.1 2.2 copy-done.6
  156.3 65.0 %image_sums.2 = (f32[32,256,256]{2,1,0:T(8,128)S(1)}, f32[32,256,256]{2,1,0:T(8,128)}, f32[32,256,256]{2,1,0:T(8,128)}, f32[32,256,256]{2,1,0:T(8,128)}, f32[16,256]{1,0:T(8,128)S(1)}, /*index=5*/f32[16,256]{1,0:T(8,128)S(1)}) custom-call(s32[64]{0:T(128)S(1)} %get-tuple-element.30.order, s32[64]{0:T(128)S(1)} %get-tuple-element.29.tile, ...), custom_call_target="tpu_custom_call" | custom-call | tf_op jit(solution)/shard_map/image_sums/pallas_call | solution.py:147
  221.3 0.0 copy-start.3
  221.3 3.2 copy-done.3
  224.5 0.7 reduce_sum.122
  225.2 0.6 reduce_sum.123
  225.8 1.3 pad_maximum_fusion
  227.1 0.1 broadcast_in_dim.97
  227.2 0.1 broadcast_in_dim.98
  227.3 0.7 broadcast_in_dim.99.part
  227.9 10.8 %total.2 = f32[8,128]{1,0:T(8,128)} custom-call(f32[8,128]{1,0:T(8,128)} %broadcast_in_dim.99.part), custom_call_target="tpu_custom_call" | custom-call | tf_op jit(solution)/shard_map/total/pallas_call | solution.py:310
  238.7 1.3 fusion.7
  241.2 35.2 %data_part.2 = f32[32,256,256]{2,1,0:T(8,128)S(1)} custom-call(s32[32]{0:T(128)S(1)} %broadcast_select_fusion.slot, s32[32]{0:T(128)S(1)} %convert_element_type.26.seen, f32[1]{0:T(128)} %bitcast.6.albedo, s32[33]{0:T(128)S(1)} %convert_reduce_fusion.1.shot_start, s32[256]{0:T(256)S(1)} %select_reduce_fusion.1.shot_pixel, ...), custom_call_target="tpu_custom_call" | custom-call | tf_op jit(solution)/shard_map/data_part/pallas_call | solution.py:215
  276.5 0.0 copy-start.5
  276.5 3.2 copy-done.5
  279.7 35.2 %add_parts.2.data = f32[256,256]{1,0:T(8,128)} custom-call(f32[2,2,4,2,256,256]{5,4,3,2,1,0:T(8,128)} %bitcast.37), custom_call_target="tpu_custom_call" | custom-call | tf_op jit(solution)/shard_map/add_parts/pallas_call | solution.py:451
  314.9 0.0 copy-start
  314.9 3.4 copy-done
  318.3 0.0 copy-start.9
  318.3 0.9 copy-done.9
  319.3 1.0 update.2
  320.3 0.0 all-gather.11.cloned.1.call-update
  320.3 77.2 %all-gather.11.cloned.1.call-done = f32[8192,256]{1,0:T(8,128)} async-done(((f32[256,256]{1,0:T(8,128)}), f32[8192,256]{1,0:T(8,128)}) %all-gather.11.cloned.1.call-update) | async-done | bytes 8388624 | tf_op jit(solution)/shard_map/all_gather | solution.py:529
  397.5 2.2 copy-done.7
  399.7 65.0 %image_sums.3 = (f32[32,256,256]{2,1,0:T(8,128)S(1)}, f32[32,256,256]{2,1,0:T(8,128)}, f32[32,256,256]{2,1,0:T(8,128)}, f32[32,256,256]{2,1,0:T(8,128)}, f32[16,256]{1,0:T(8,128)S(1)}, /*index=5*/f32[16,256]{1,0:T(8,128)S(1)}) custom-call(s32[64]{0:T(128)S(1)} %get-tuple-element.30.order, s32[64]{0:T(128)S(1)} %get-tuple-element.29.tile, ...), custom_call_target="tpu_custom_call" | custom-call | tf_op jit(solution)/shard_map/image_sums/pallas_call | solution.py:147
  464.7 3.2 copy-done.2
  467.9 0.6 reduce_sum.128
  468.5 0.6 reduce_sum.129
  469.1 1.3 pad_maximum_fusion.1
  470.4 0.1 broadcast_in_dim.104
  470.4 0.1 broadcast_in_dim.105
  470.5 0.7 broadcast_in_dim.106.part
  471.2 10.8 %total.3 = f32[8,128]{1,0:T(8,128)} custom-call(f32[8,128]{1,0:T(8,128)} %broadcast_in_dim.106.part), custom_call_target="tpu_custom_call" | custom-call | tf_op jit(solution)/shard_map/total/pallas_call | solution.py:310
  482.0 1.3 fusion.6
  484.7 35.2 %data_part.3 = f32[32,256,256]{2,1,0:T(8,128)S(1)} custom-call(s32[32]{0:T(128)S(1)} %broadcast_select_fusion.slot, s32[32]{0:T(128)S(1)} %convert_element_type.26.seen, f32[1]{0:T(128)} %bitcast.12.albedo, s32[33]{0:T(128)S(1)} %convert_reduce_fusion.1.shot_start, s32[256]{0:T(256)S(1)} %select_reduce_fusion.1.shot_pixel, ...), custom_call_target="tpu_custom_call" | custom-call | tf_op jit(solution)/shard_map/data_part/pallas_call | solution.py:215
  519.9 0.0 copy-start.4
  519.9 3.2 copy-done.4
  523.1 35.2 %add_parts.3.data = f32[256,256]{1,0:T(8,128)} custom-call(f32[2,2,4,2,256,256]{5,4,3,2,1,0:T(8,128)} %bitcast.36), custom_call_target="tpu_custom_call" | custom-call | tf_op jit(solution)/shard_map/add_parts/pallas_call | solution.py:451
  558.4 0.0 copy-start.1
  558.4 3.4 copy-done.1
  561.7 0.9 copy-done.8
  562.7 1.0 update.3
  (5 shorter events, 0.0 us)
Async XLA Ops:
  6.5 68.7 %all-gather.9.cloned.1.call-start = ((), (), s32[]{:S(2)}) async-start(), calls=%async_computation.1 | async-start | bytes 4325376 | tf_op jit(solution)/shard_map/all_gather | solution.py:525
  8.2 145.9 %all-gather.7.cloned.1.call-start = ((), (), s32[]{:S(2)}) async-start(), calls=%async_computation | async-start | bytes 8650752 | tf_op jit(solution)/shard_map/all_gather | solution.py:529
  8.9 388.5 %all-gather.11.cloned.1.call-start = ((), (), s32[]{:S(2)}) async-start(), calls=%async_computation.2 | async-start | bytes 8650752 | tf_op jit(solution)/shard_map/all_gather | solution.py:529
  154.1 2.2 copy-start.6
  221.3 3.2 copy-start.3
  276.5 3.2 copy-start.5
  314.9 3.4 copy-start
  318.3 0.9 copy-start.9
  397.5 2.2 copy-start.7
  464.7 3.2 copy-start.2
  519.9 3.2 copy-start.4
  558.4 3.4 copy-start.1
  561.7 0.9 copy-start.8
Sparse Core Ops, SparseCore 0:
  10.4 64.7 all-gather.8
  78.2 75.8 all-gather.6
  320.4 77.0 all-gather.10

commit v3 on v2

--- a/solution.py
+++ b/solution.py
@@ -19,9 +19,10 @@
 LOG2E = math.log2(math.e)
 CHUNK = 16
 LINK = jnp.bfloat16
-
-
-def rim_specs(side, cols, tiles, tile_of):
+VMEM_BYTES = 60 * 2**20
+
+
+def rim_specs(side, cols, tiles, tile_of, high=8):
     def at(offset, block, where):
         def index(*args):
             tile = jnp.clip(tile_of(*args) + offset, 0, tiles - 1)
@@ -31,8 +32,8 @@
 
     return [
         at(0, (side, side), (0, 0)),
-        at(-cols, (8, side), (side // 8 - 1, 0)),
-        at(cols, (8, side), (0, 0)),
+        at(-cols, (high, side), (side // high - 1, 0)),
+        at(cols, (high, side), (0, 0)),
         at(-1, (side, 128), (0, side // 128 - 1)),
         at(1, (side, 128), (0, 0)),
     ]
@@ -56,10 +57,10 @@
 
 
 def image_kernel(
-    rows, cols, order, tile, slot, first, last, sun,
+    rows, cols, order, tile, start, sun,
     pixels, center, up, down, left, right, lit,
-    obs_x, obs_y, fit_x, fit_y, cross, power,
-    inv_s, px_s, py_s, ox_s, oy_s, fx_s, fy_s,
+    obs_x, obs_y, fit_x, fit_y, part,
+    inv_s, px_s, py_s, ox_s, oy_s, fx_s, fy_s, cross, power,
 ):
     i = pl.program_id(0)
     side = center.shape[1]
@@ -69,7 +70,7 @@
         cross[...] = jnp.zeros_like(cross)
         power[...] = jnp.zeros_like(power)
 
-    @pl.when(first[i] == 1)
+    @pl.when(start[i + 1] > start[i])
     def start_tile():
         g_up, g_down, g_left, g_right = edges(tile[i], rows, cols)
         above, below, before, after = shifted(
@@ -85,24 +86,12 @@
         inv_s[...] = inverse
         px_s[...] = slope_x * inverse
         py_s[...] = slope_y * inverse
-        zero = jnp.zeros((side, side), jnp.float32)
-        ox_s[...] = zero
-        oy_s[...] = zero
-        fx_s[...] = zero
-        fy_s[...] = zero
-
-    k = order[i]
-    sx, sy, sz, gain = sun[4 * k], sun[4 * k + 1], sun[4 * k + 2], sun[4 * k + 3]
-    scale = sharpness * LOG2E
-    ux, uy, uz = sx * scale, sy * scale, sz * scale
-    refl_scale = gain * (1.0 / (sharpness * LOG2E))
-    gx, gy = gain * sx, gain * sy
-    gc = gain * (1.0 / scale)
-
-    def step(j, sums):
+
+    def step(fresh, numbers, j, sums):
+        k, ux, uy, uz, refl_scale, gx, gy, gc = numbers
         at = pl.ds(pl.multiple_of(j * CHUNK, CHUNK), CHUNK)
         inverse, px, py = inv_s[at, :], px_s[at, :], py_s[at, :]
-        observed = pixels[0, at, :].astype(jnp.float32)
+        observed = pixels[k, at, :].astype(jnp.float32)
         shine = lit[0, at, :].astype(jnp.float32)
         u = uz * inverse - ux * px - uy * py
         soft = jnp.log2(1.0 + jnp.exp2(u))
@@ -113,19 +102,36 @@
         dy = gy + v * py
         seen = sigma * observed
         model = sigma * q
-        ox_s[at, :] += seen * dx
-        oy_s[at, :] += seen * dy
-        fx_s[at, :] += model * dx
-        fy_s[at, :] += model * dy
+        for held, term in (
+            (ox_s, seen * dx), (oy_s, seen * dy), (fx_s, model * dx), (fy_s, model * dy)
+        ):
+            held[at, :] = term if fresh else held[at, :] + term
         shone = shine * q
         return sums[0] + shone * observed, sums[1] + shone * q
 
-    zero = jnp.zeros((CHUNK, side), jnp.float32)
-    sums = lax.fori_loop(0, side // CHUNK, step, (zero, zero), unroll=2)
-    cross[...] += sums[0]
-    power[...] += sums[1]
-
-    @pl.when(last[i] == 1)
+    def sweep(fresh, n):
+        k = order[n]
+        sx, sy, sz, gain = sun[4 * k], sun[4 * k + 1], sun[4 * k + 2], sun[4 * k + 3]
+        scale = sharpness * LOG2E
+        numbers = (
+            k, sx * scale, sy * scale, sz * scale,
+            gain * (1.0 / scale), gain * sx, gain * sy, gain * (1.0 / scale),
+        )
+        zero = jnp.zeros((CHUNK, side), jnp.float32)
+        sums = lax.fori_loop(
+            0, side // CHUNK, functools.partial(step, fresh, numbers), (zero, zero), unroll=2
+        )
+        cross[...] += sums[0]
+        power[...] += sums[1]
+
+    def more(n, carry):
+        sweep(False, n)
+        return carry
+
+    pl.when(start[i + 1] > start[i])(lambda: sweep(True, start[i]))
+    lax.fori_loop(start[i] + 1, start[i + 1], more, 0)
+
+    @pl.when(start[i + 1] > start[i])
     def end_tile():
         factor = inv_s[...] * (-lit[0].astype(jnp.float32))
         obs_x[0] = (ox_s[...] * factor).astype(obs_x.dtype)
@@ -133,32 +139,42 @@
         fit_x[0] = (fx_s[...] * factor).astype(fit_x.dtype)
         fit_y[0] = (fy_s[...] * factor).astype(fit_y.dtype)
 
+    @pl.when(i == pl.num_programs(0) - 1)
+    def end_sums():
+        for n, held in enumerate((cross, power)):
+            total = jnp.zeros((8, 128), jnp.float32)
+            for a in range(CHUNK // 8):
+                for b in range(side // 128):
+                    total = total + held[8 * a : 8 * a + 8, 128 * b : 128 * b + 128]
+            part[8 * n : 8 * n + 8, :] = total
+
 
 def image_sums(rows, cols, plan, sun, pixels, surface_all, lit_all):
-    order, tile, slot, first, last = plan
+    order, tile, start = plan
     images, side = pixels.shape[0], pixels.shape[1]
     tiles = rows * cols
     slots = min(tiles, images)
     by_tile = lambda i, order, tile, *rest: tile[i]
-    field = jax.ShapeDtypeStruct((slots, side, side), jnp.float32)
-    part = jax.ShapeDtypeStruct((CHUNK, side), jnp.float32)
-    field_spec = pl.BlockSpec((1, side, side), lambda i, order, tile, slot, *rest: (slot[i], 0, 0))
-    part_spec = pl.BlockSpec((CHUNK, side), lambda i, *rest: (0, 0))
+    field = jax.ShapeDtypeStruct((slots, side, side), jnp.bfloat16)
+    part = jax.ShapeDtypeStruct((16, 128), jnp.float32)
+    field_spec = pl.BlockSpec((1, side, side), lambda i, *rest: (i, 0, 0))
+    part_spec = pl.BlockSpec((16, 128), lambda i, *rest: (0, 0))
     return pl.pallas_call(
         functools.partial(image_kernel, rows, cols),
-        out_shape=[field] * 4 + [part] * 2,
+        out_shape=[field] * 4 + [part],
         grid_spec=pltpu.PrefetchScalarGridSpec(
-            num_scalar_prefetch=6,
-            grid=(images,),
-            in_specs=[pl.BlockSpec((1, side, side), lambda i, order, *rest: (order[i], 0, 0))]
+            num_scalar_prefetch=4,
+            grid=(slots,),
+            in_specs=[pl.BlockSpec(memory_space=pltpu.VMEM)]
             + rim_specs(side, cols, tiles, by_tile)
             + [pl.BlockSpec((1, side, side), lambda i, order, tile, *rest: (tile[i], 0, 0))],
-            out_specs=[field_spec] * 4 + [part_spec] * 2,
-            scratch_shapes=[pltpu.VMEM((side, side), jnp.float32)] * 7,
+            out_specs=[field_spec] * 4 + [part_spec],
+            scratch_shapes=[pltpu.VMEM((side, side), jnp.float32)] * 7
+            + [pltpu.VMEM((CHUNK, side), jnp.float32)] * 2,
         ),
-        compiler_params=pltpu.CompilerParams(vmem_limit_bytes=40 * 2**20),
+        compiler_params=pltpu.CompilerParams(vmem_limit_bytes=VMEM_BYTES),
         name="image_sums",
-    )(order, tile, slot, first, last, sun, pixels, *([surface_all] * 5), lit_all)
+    )(order, tile, start, sun, pixels, *([surface_all] * 5), lit_all)
 
 
 def data_kernel(
@@ -172,14 +188,14 @@
     has = lambda n: jnp.where(seen[jnp.clip(n, 0, tiles - 1)] == 1, a, 0.0)
     here, above, below = has(t), has(t - cols) * g_up, has(t + cols) * g_down
     before, after = has(t - 1) * g_left, has(t + 1) * g_right
-    mix = lambda f, o, gate: (a * f - o) * gate
+    mix = lambda f, o, gate: (a * f.astype(jnp.float32) - o.astype(jnp.float32)) * gate
     grad_x = mix(fx[0], ox[0], here)
     grad_y = mix(fy[0], oy[0], here)
     side = grad_x.shape[0]
-    left = mix(fx_l[0, :, 127:128], ox_l[0, :, 127:128], before)
-    right = mix(fx_r[0, :, 0:1], ox_r[0, :, 0:1], after)
-    up = mix(fy_u[0, 7:8, :], oy_u[0, 7:8, :], above)
-    down = mix(fy_d[0, 0:1, :], oy_d[0, 0:1, :], below)
+    left = mix(fx_l[0], ox_l[0], before)[:, 127:128]
+    right = mix(fx_r[0], ox_r[0], after)[:, 0:1]
+    up = mix(fy_u[0], oy_u[0], above)[15:16, :]
+    down = mix(fy_d[0], oy_d[0], below)[0:1, :]
     row = lax.broadcasted_iota(jnp.int32, grad_x.shape, 0)
     col = lax.broadcasted_iota(jnp.int32, grad_x.shape, 1)
     y_above = jnp.where(row == 0, up, pltpu.roll(grad_y, 1, 0))
@@ -202,7 +218,7 @@
 def data_part(rows, cols, slot, seen, albedo, shots, surface_all, obs_x, obs_y, fit_x, fit_y):
     side = obs_x.shape[1]
     tiles = rows * cols
-    center, up, down, left, right = rim_specs(side, cols, tiles, lambda t, *rest: t)
+    center, up, down, left, right = rim_specs(side, cols, tiles, lambda t, *rest: t, 16)
 
     def through(spec):
         def index(t, slot, *rest):
@@ -223,7 +239,7 @@
             + [pl.BlockSpec((1, side, side), lambda t, *rest: (t, 0, 0))],
             out_specs=pl.BlockSpec((1, side, side), lambda t, *rest: (t, 0, 0)),
         ),
-        compiler_params=pltpu.CompilerParams(vmem_limit_bytes=40 * 2**20),
+        compiler_params=pltpu.CompilerParams(vmem_limit_bytes=VMEM_BYTES),
         name="data_part",
     )(
         slot, seen, albedo, *shots,
@@ -258,7 +274,7 @@
             in_specs=rim_specs(side, cols, rows * cols, lambda i, me: me[0]) + [whole],
             out_specs=whole,
         ),
-        compiler_params=pltpu.CompilerParams(vmem_limit_bytes=40 * 2**20),
+        compiler_params=pltpu.CompilerParams(vmem_limit_bytes=VMEM_BYTES),
         name="update",
     )(me, *([surface_all] * 5), data)
 
@@ -302,14 +318,15 @@
     held[0] = part[...]
     lax.fori_loop(1, devices, send, 0)
     lax.fori_loop(1, devices, land, 0)
-    total[...] = jnp.sum(held[...], axis=0)
+    sums = jnp.sum(held[...], axis=0)
+    total[...] = jnp.full(total.shape, jnp.sum(sums[:8]) / jnp.sum(sums[8:]), jnp.float32)
 
 
 def total_over_devices(rows, cols, part):
     devices = rows * cols
     return pl.pallas_call(
         functools.partial(total_kernel, rows, cols),
-        out_shape=jax.ShapeDtypeStruct(part.shape, jnp.float32),
+        out_shape=jax.ShapeDtypeStruct((8, 128), jnp.float32),
         in_specs=[pl.BlockSpec(memory_space=pltpu.VMEM)],
         out_specs=pl.BlockSpec(memory_space=pltpu.VMEM),
         scratch_shapes=[
@@ -317,7 +334,9 @@
             pltpu.SemaphoreType.DMA((devices,)),
             pltpu.SemaphoreType.DMA((devices,)),
         ],
-        compiler_params=pltpu.CompilerParams(collective_id=0, has_side_effects=True),
+        compiler_params=pltpu.CompilerParams(
+            collective_id=0, has_side_effects=True, vmem_limit_bytes=VMEM_BYTES
+        ),
         name="total",
     )(part)
 
@@ -473,10 +492,121 @@
             dma((Z - 1,)),
         ],
         compiler_params=pltpu.CompilerParams(
-            collective_id=1, has_side_effects=True, vmem_limit_bytes=56 * 2**20
+            collective_id=1, has_side_effects=True, vmem_limit_bytes=VMEM_BYTES
         ),
         name="add_parts",
     )(data.reshape(X, 2, Z, 2, side, side))
+
+
+def gather_kernel(rows, cols, count, *refs):
+    mine, outs = refs[:count], refs[count : 2 * count]
+    local_sem, sz, rz, sa, ra, sb, rb, sc, rc = refs[2 * count :]
+    X, Z = rows // 2, cols // 2
+    side = mine[0].shape[0]
+    half = side // 2
+    r, c = lax.axis_index("row"), lax.axis_index("col")
+    x, k, z, y = r // 2, lax.rem(r, 2), c // 2, lax.rem(c, 2)
+    core_peer = (x * 2 + 1 - k, c)
+    x_peers = [(lax.rem(x + d, X) * 2 + k, c) for d in range(1, X)]
+    y_peers = [(r, z * 2 + 1 - y)]
+    z_peers = [(r, lax.rem(z + d, Z) * 2 + y) for d in range(1, Z)]
+    source = [lax.rem(z + Z - d, Z) for d in range(Z)]
+
+    barrier = pltpu.get_barrier_semaphore()
+    peers = [core_peer] + x_peers + y_peers + z_peers
+    for peer in peers:
+        pl.semaphore_signal(barrier, inc=1, device_id=peer, device_id_type=pl.DeviceIdType.MESH)
+    pl.semaphore_wait(barrier, len(peers))
+
+    def remote(src, dst, send, recv, peer):
+        return pltpu.make_async_remote_copy(
+            src_ref=src, dst_ref=dst, send_sem=send, recv_sem=recv,
+            device_id=peer, device_id_type=pl.DeviceIdType.MESH,
+        )
+
+    own = [pltpu.make_async_copy(mine[n], outs[n].at[x, k, z, y], local_sem.at[n]) for n in range(count)]
+    streams = []
+    for n in range(count):
+        own[n].start()
+        for h in range(2):
+            part = pl.ds(h * half, half)
+            s = 2 * n + h
+            along_z = [
+                remote(
+                    mine[n].at[part], outs[n].at[x, k, z, y, part],
+                    sz.at[s, d], rz.at[s, d], z_peers[d],
+                )
+                for d in range(Z - 1)
+            ]
+            a_peers, b_peers = (x_peers, y_peers) if h else (y_peers, x_peers)
+            along_a, along_b, along_core = [], [], []
+            for e in range(Z):
+                tile = outs[n].at[x, k, source[e], y, part]
+                slab = outs[n].at[:, k, source[e], y, part] if h else outs[n].at[x, k, source[e], :, part]
+                full = outs[n].at[:, k, source[e], :, part]
+                along_a.append(
+                    [
+                        remote(tile, tile, sa.at[s, e, d], ra.at[s, e, d], peer)
+                        for d, peer in enumerate(a_peers)
+                    ]
+                )
+                along_b.append(
+                    [
+                        remote(slab, slab, sb.at[s, e, d], rb.at[s, e, d], peer)
+                        for d, peer in enumerate(b_peers)
+                    ]
+                )
+                along_core.append(remote(full, full, sc.at[s, e], rc.at[s, e], core_peer))
+            for copy in along_z:
+                copy.start()
+            streams.append((along_z, along_a, along_b, along_core))
+    for copy in own:
+        copy.wait()
+    for t in range(Z + 2):
+        for along_z, along_a, along_b, along_core in streams:
+            if t < Z:
+                if t:
+                    along_z[t - 1].wait_recv()
+                for copy in along_a[t]:
+                    copy.start()
+            if 0 <= t - 1 < Z:
+                for copy in along_a[t - 1]:
+                    copy.wait_recv()
+                for copy in along_b[t - 1]:
+                    copy.start()
+            if 0 <= t - 2 < Z:
+                for copy in along_b[t - 2]:
+                    copy.wait_recv()
+                along_core[t - 2].start()
+    for along_z, along_a, along_b, along_core in streams:
+        for copy in along_core:
+            copy.wait_recv()
+        for copy in along_z + sum(along_a, []) + sum(along_b, []) + along_core:
+            copy.wait_send()
+
+
+def gather(rows, cols, values, collective):
+    X, Z = rows // 2, cols // 2
+    count, most = len(values), max(X - 1, 1)
+    side = values[0].shape[0]
+    anywhere = pl.BlockSpec(memory_space=pl.ANY)
+    dma = pltpu.SemaphoreType.DMA
+    streams = 2 * count
+    outs = pl.pallas_call(
+        functools.partial(gather_kernel, rows, cols, count),
+        out_shape=[jax.ShapeDtypeStruct((X, 2, Z, 2, side, side), v.dtype) for v in values],
+        in_specs=[anywhere] * count,
+        out_specs=[anywhere] * count,
+        scratch_shapes=[dma((count,))]
+        + [dma((streams, Z - 1))] * 2
+        + [dma((streams, Z, most))] * 4
+        + [dma((streams, Z))] * 2,
+        compiler_params=pltpu.CompilerParams(
+            collective_id=collective, has_side_effects=True, vmem_limit_bytes=VMEM_BYTES
+        ),
+        name="gather",
+    )(*values)
+    return [out.reshape(rows * cols, side, side) for out in outs]
 
 
 def image_plan(dest, tiles):
@@ -488,18 +618,16 @@
     rank = jnp.sum(earlier, axis=1)
     chosen = rank[None, :] == place[:, None]
     order = jnp.sum(jnp.where(chosen, place[None, :], 0), axis=1).astype(jnp.int32)
-    tile = jnp.sum(jnp.where(chosen, dest[None, :], 0), axis=1).astype(jnp.int32)
     seen = jnp.any(dest[None, :] == jnp.arange(tiles)[:, None], axis=1)
     before = jnp.arange(tiles)[None, :] < jnp.arange(tiles)[:, None]
     tile_slot = jnp.where(seen, jnp.sum(before & seen[None, :], axis=1), 0).astype(jnp.int32)
-    slot = jnp.sum(
-        jnp.where(tile[:, None] == jnp.arange(tiles)[None, :], tile_slot[None, :], 0), axis=1
-    ).astype(jnp.int32)
-    change = (tile[1:] != tile[:-1]).astype(jnp.int32)
-    one = jnp.ones((1,), jnp.int32)
-    first = jnp.concatenate([one, change])
-    last = jnp.concatenate([change, one])
-    return (order, tile, slot, first, last), tile_slot, seen.astype(jnp.int32)
+    slots = jnp.arange(min(tiles, count) + 1)
+    held = seen[None, :] & (tile_slot[None, :] == slots[:-1, None])
+    slot_tile = jnp.sum(jnp.where(held, jnp.arange(tiles)[None, :], 0), axis=1).astype(jnp.int32)
+    named = jnp.sum(dest[None, :] == jnp.arange(tiles)[:, None], axis=1)
+    past = seen[None, :] & (tile_slot[None, :] < slots[:, None])
+    start = jnp.sum(jnp.where(past, named[None, :], 0), axis=1).astype(jnp.int32)
+    return (order, slot_tile, start), tile_slot, seen.astype(jnp.int32)
 
 
 def shot_plan(dest, pixel, height, tiles):
@@ -522,18 +650,18 @@
     me = (lax.axis_index("row") * cols + lax.axis_index("col")).astype(jnp.int32).reshape(1)
     plan, tile_slot, seen = image_plan(image_dest[:, 0], tiles)
     sun = sun_gain.astype(jnp.float32).reshape(-1)
-    lit_all = lax.all_gather((1.0 - shadow.astype(jnp.float32)).astype(jnp.bfloat16), AXES)
+    lit = (1 - shadow).astype(jnp.bfloat16)
     shots = shot_plan(shot_dest[:, 0], shot_pixel, shot_height, tiles)
     surface = heights
     for sweep in range(ITERS):
-        surface_all = lax.all_gather(surface, AXES)
-        obs_x, obs_y, fit_x, fit_y, cross, power = image_sums(
+        if sweep == 0:
+            surface_all, lit_all = gather(rows, cols, [surface, lit], 2)
+        else:
+            (surface_all,) = gather(rows, cols, [surface], 3)
+        obs_x, obs_y, fit_x, fit_y, part = image_sums(
             rows, cols, plan, sun, image_tiles, surface_all, lit_all
         )
-        sums = jnp.stack([jnp.sum(cross), jnp.sum(power)])
-        sums = jnp.broadcast_to(sums[:, None, None], (2, 4, 128)).reshape(8, 128)
-        sums = total_over_devices(rows, cols, sums)
-        albedo = (sums[0, 0] / sums[4, 0]).reshape(1)
+        albedo = total_over_devices(rows, cols, part)[0, :1]
         data = data_part(
             rows, cols, tile_slot, seen, albedo, shots, surface_all, obs_x, obs_y, fit_x, fit_y
         )

time: 574 us -> 418 us (0.73)
  waiting for transfers between devices: 216 us -> 0 us
  Pallas kernels: 295 us -> 402 us
  local copies, waits for them, and re-layouts: 31 us -> 3.8 us
  between operations: 15.8 us -> 0.1 us
    all_gather x3 -> x0, waiting for transfers between devices: 215 us -> none  [the longest x2 156 us: body(): surface_all = lax.all_gather(surface, AXES)]
    pallas_call x0 -> x2, Pallas kernels: none -> 127 us  [gather(): pl.pallas_call(functools.partial(gather_kernel, rows, cols, count), out_s...]
    pallas_call x2, Pallas kernels: 130 us -> 101 us  [image_sums(): pl.pallas_call(functools.partial(image_kernel, rows, cols), out_shape=[fi...]
    unnamed x20 -> x8, local copies, waits for them, and re-layouts: 25.8 us -> 0.02 us
    pallas_call x2, Pallas kernels: 21.6 us -> 32.4 us  [total_over_devices(): pl.pallas_call(functools.partial(total_kernel, rows, cols), out_shape=jax...]
  transfers between devices with their start and end apart: 3 -> 0, of which waited for: 3 -> 0; matrix products, arithmetic and copies ran while one was open for 1% -> 0% of each run, Pallas kernels for 0% -> 0%
where the time goes in v3:
time: 418 us; the launch traced here: 415 us
  Pallas kernels  402 us (96%)
  other arithmetic  9.03 us (2%)
    pallas_call x2, Pallas kernels, gather(): pl.pallas_call(functools.partial(gather_kernel, rows, cols, count), out_s...  127 us
    pallas_call x2, Pallas kernels, image_sums(): pl.pallas_call(functools.partial(image_kernel, rows, cols), out_shape=[fi...  101 us
    pallas_call x2, Pallas kernels, add_parts(): pl.pallas_call(functools.partial(add_kernel, rows, cols), out_shape=jax.S...  71.4 us
    pallas_call x2, Pallas kernels, data_part(): pl.pallas_call(functools.partial(data_kernel, rows, cols), out_shape=jax....  65.1 us
    pallas_call x2, Pallas kernels, total_over_devices(): pl.pallas_call(functools.partial(total_kernel, rows, cols), out_shape=jax...  32.4 us

profile of v3, /device:TPU:0, one launch (start us, length us, event | category | flops | bytes accessed | tf_op | source)
XLA Modules:
  0.0 415.0 jit_solution(8144868699890482227)
XLA Ops:
  0.0 0.8 fusion.4
  0.8 0.1 convert_reduce_fusion.4
  0.9 0.0 copy-start
  0.9 0.8 convert_reduce_fusion.3
  1.7 0.7 select_reduce_fusion.3.start
  2.4 0.7 select_reduce_fusion.4.tile
  3.1 1.6 subtract_convert_fusion.refs_1_
  4.7 74.1 %gather.2 = (f32[2,2,4,2,256,256]{5,4,3,2,1,0:T(8,128)}, bf16[2,2,4,2,256,256]{5,4,3,2,1,0:T(8,128)(2,1)}) custom-call(f32[256,256]{1,0:T(8,128)} %refs_0_.1, bf16[256,256]{1,0:T(8,128)(2,1)} %subtract_convert_fusion.refs_1_), custom_call_target="tpu_custom_call" | custom-call | tf_op jit(solution)/shard_map/gather/pallas_call | solution.py:595
  78.9 0.9 convert_reduce_fusion.2
  79.8 0.7 select_reduce_fusion.2.order
  80.5 0.8 copy.10
  81.2 0.6 reshape.46.sun
  81.9 0.0 copy-start.1
  81.9 0.0 copy-start.2
  81.9 0.0 copy-start.3
  81.9 50.8 %image_sums.2 = (bf16[32,256,256]{2,1,0:T(8,128)(2,1)}, bf16[32,256,256]{2,1,0:T(8,128)(2,1)}, bf16[32,256,256]{2,1,0:T(8,128)(2,1)}, bf16[32,256,256]{2,1,0:T(8,128)(2,1)}, f32[16,128]{1,0:T(8,128)}) custom-call(s32[64]{0:T(128)} %select_reduce_fusion.2.order, s32[32]{0:T(128)} %select_reduce_fusion.4.tile, s32[33]{0:T(128)} %select_reduce_fusion.3.start, ...), custom_call_target="tpu_custom_call" | custom-call | tf_op jit(solution)/shard_map/image_sums/pallas_call | solution.py:162
  132.7 0.0 copy-done
  132.7 18.4 %total.2 = f32[8,128]{1,0:T(8,128)} custom-call(f32[16,128]{1,0:T(8,128)} %get-tuple-element.19.part), custom_call_target="tpu_custom_call" | custom-call | tf_op jit(solution)/shard_map/total/pallas_call | solution.py:327
  151.1 1.2 slice.10
  152.2 0.6 convert_element_type.24.seen
  152.8 0.0 copy-done.1
  152.8 0.2 convert_reduce_fusion
  153.0 0.0 copy-done.2
  153.0 0.7 select_reduce_fusion.shot_height
  153.7 0.0 copy-done.3
  153.7 0.6 select_reduce_fusion.1.shot_pixel
  154.3 0.7 convert_reduce_fusion.1.shot_start
  155.0 32.5 %data_part.2 = f32[32,256,256]{2,1,0:T(8,128)} custom-call(s32[32]{0:T(128)} %copy-done, s32[32]{0:T(128)} %convert_element_type.24.seen, f32[1]{0:T(128)} %bitcast.4.albedo, s32[33]{0:T(128)} %convert_reduce_fusion.1.shot_start, s32[256]{0:T(256)} %select_reduce_fusion.1.shot_pixel, f32[256]{0:T(256)} %select_reduce_fusion.shot_height, ...), custom_call_target="tpu_custom_call" | custom-call | tf_op jit(solution)/shard_map/data_part/pallas_call | solution.py:231
  187.5 35.7 %add_parts.2.data = f32[256,256]{1,0:T(8,128)} custom-call(f32[2,2,4,2,256,256]{5,4,3,2,1,0:T(8,128)} %bitcast.34), custom_call_target="tpu_custom_call" | custom-call | tf_op jit(solution)/shard_map/add_parts/pallas_call | solution.py:470
  223.2 2.2 update.2.refs_0_
  225.4 53.2 %gather.3 = f32[2,2,4,2,256,256]{5,4,3,2,1,0:T(8,128)} custom-call(f32[256,256]{1,0:T(8,128)} %update.2.refs_0_), custom_call_target="tpu_custom_call" | custom-call | tf_op jit(solution)/shard_map/gather/pallas_call | solution.py:595
  278.6 50.7 %image_sums.3 = (bf16[32,256,256]{2,1,0:T(8,128)(2,1)}, bf16[32,256,256]{2,1,0:T(8,128)(2,1)}, bf16[32,256,256]{2,1,0:T(8,128)(2,1)}, bf16[32,256,256]{2,1,0:T(8,128)(2,1)}, f32[16,128]{1,0:T(8,128)}) custom-call(s32[64]{0:T(128)} %select_reduce_fusion.2.order, s32[32]{0:T(128)} %select_reduce_fusion.4.tile, s32[33]{0:T(128)} %select_reduce_fusion.3.start, ...), custom_call_target="tpu_custom_call" | custom-call | tf_op jit(solution)/shard_map/image_sums/pallas_call | solution.py:162
  329.3 14.0 %total.3 = f32[8,128]{1,0:T(8,128)} custom-call(f32[16,128]{1,0:T(8,128)} %get-tuple-element.24.part), custom_call_target="tpu_custom_call" | custom-call | tf_op jit(solution)/shard_map/total/pallas_call | solution.py:327
  343.4 1.2 slice.11
  344.5 32.5 %data_part.3 = f32[32,256,256]{2,1,0:T(8,128)} custom-call(s32[32]{0:T(128)} %copy-done, s32[32]{0:T(128)} %convert_element_type.24.seen, f32[1]{0:T(128)} %bitcast.8.albedo, s32[33]{0:T(128)} %convert_reduce_fusion.1.shot_start, s32[256]{0:T(256)} %select_reduce_fusion.1.shot_pixel, f32[256]{0:T(256)} %select_reduce_fusion.shot_height, ...), custom_call_target="tpu_custom_call" | custom-call | tf_op jit(solution)/shard_map/data_part/pallas_call | solution.py:231
  377.1 35.7 %add_parts.3.data = f32[256,256]{1,0:T(8,128)} custom-call(f32[2,2,4,2,256,256]{5,4,3,2,1,0:T(8,128)} %bitcast.33), custom_call_target="tpu_custom_call" | custom-call | tf_op jit(solution)/shard_map/add_parts/pallas_call | solution.py:470
  412.8 2.2 update.3
  (2 shorter events, 0.0 us)
Async XLA Ops:
  0.9 131.8 %copy-start = (s32[32]{0:T(128)}, s32[32]{0:T(128)S(1)}, u32[]{:S(2)}) copy-start(s32[32]{0:T(128)S(1)} %broadcast_select_fusion.slot) | copy-start | bytes 388
  81.9 71.0 %copy-start.1 = (s32[256,1]{0,1:T(1,128)S(1)}, s32[256,1]{0,1:T(1,128)}, u32[]{:S(2)}) copy-start(s32[256,1]{0,1:T(1,128)} %param.13) | copy-start | bytes 3076
  81.9 71.1 %copy-start.2 = (f32[256]{0:T(256)S(1)}, f32[256]{0:T(256)}, u32[]{:S(2)}) copy-start(f32[256]{0:T(256)} %param.15) | copy-start | bytes 3076
  81.9 71.8 %copy-start.3 = (s32[256]{0:T(256)S(1)}, s32[256]{0:T(256)}, u32[]{:S(2)}) copy-start(s32[256]{0:T(256)} %param.14) | copy-start | bytes 3076

commit v4 on v3

--- a/solution.py
+++ b/solution.py
@@ -73,19 +73,34 @@
     @pl.when(start[i + 1] > start[i])
     def start_tile():
         g_up, g_down, g_left, g_right = edges(tile[i], rows, cols)
-        above, below, before, after = shifted(
-            center[0],
-            up[0, 7:8, :] * g_up,
-            down[0, 0:1, :] * g_down,
-            left[0, :, 127:128] * g_left,
-            right[0, :, 0:1] * g_right,
-        )
-        slope_x = (after - before) * 0.5
-        slope_y = (below - above) * 0.5
-        inverse = lax.rsqrt(1.0 + slope_x * slope_x + slope_y * slope_y)
-        inv_s[...] = inverse
-        px_s[...] = slope_x * inverse
-        py_s[...] = slope_y * inverse
+        row = lax.broadcasted_iota(jnp.int32, (CHUNK, side), 0)
+        col = lax.broadcasted_iota(jnp.int32, (CHUNK, side), 1)
+        top = up[0, 7:8, :] * g_up
+        bottom = down[0, 0:1, :] * g_down
+        chunks = side // CHUNK
+
+        def slopes(j, carry):
+            at = pl.ds(pl.multiple_of(j * CHUNK, CHUNK), CHUNK)
+            here = center[0, at, :]
+            higher = center[0, pl.ds(jnp.maximum(j * CHUNK - 1, 0), 1), :]
+            lower = center[0, pl.ds(jnp.minimum(j * CHUNK + CHUNK, side - 1), 1), :]
+            higher = jnp.where(j == 0, top, higher)
+            lower = jnp.where(j == chunks - 1, bottom, lower)
+            above = jnp.where(row == 0, higher, pltpu.roll(here, 1, 0))
+            below = jnp.where(row == CHUNK - 1, lower, pltpu.roll(here, CHUNK - 1, 0))
+            before = jnp.where(col == 0, left[0, at, 127:128] * g_left, pltpu.roll(here, 1, 1))
+            after = jnp.where(
+                col == side - 1, right[0, at, 0:1] * g_right, pltpu.roll(here, side - 1, 1)
+            )
+            slope_x = (after - before) * 0.5
+            slope_y = (below - above) * 0.5
+            inverse = lax.rsqrt(1.0 + slope_x * slope_x + slope_y * slope_y)
+            inv_s[at, :] = inverse
+            px_s[at, :] = slope_x * inverse
+            py_s[at, :] = slope_y * inverse
+            return carry
+
+        lax.fori_loop(0, chunks, slopes, 0, unroll=2)
 
     def step(fresh, numbers, j, sums):
         k, ux, uy, uz, refl_scale, gx, gy, gc = numbers
@@ -133,11 +148,14 @@
 
     @pl.when(start[i + 1] > start[i])
     def end_tile():
-        factor = inv_s[...] * (-lit[0].astype(jnp.float32))
-        obs_x[0] = (ox_s[...] * factor).astype(obs_x.dtype)
-        obs_y[0] = (oy_s[...] * factor).astype(obs_y.dtype)
-        fit_x[0] = (fx_s[...] * factor).astype(fit_x.dtype)
-        fit_y[0] = (fy_s[...] * factor).astype(fit_y.dtype)
+        def write(j, carry):
+            at = pl.ds(pl.multiple_of(j * CHUNK, CHUNK), CHUNK)
+            factor = inv_s[at, :] * (-lit[0, at, :].astype(jnp.float32))
+            for field, held in ((obs_x, ox_s), (obs_y, oy_s), (fit_x, fx_s), (fit_y, fy_s)):
+                field[0, at, :] = (held[at, :] * factor).astype(field.dtype)
+            return carry
+
+        lax.fori_loop(0, side // CHUNK, write, 0, unroll=2)
 
     @pl.when(i == pl.num_programs(0) - 1)
     def end_sums():
@@ -189,20 +207,31 @@
     here, above, below = has(t), has(t - cols) * g_up, has(t + cols) * g_down
     before, after = has(t - 1) * g_left, has(t + 1) * g_right
     mix = lambda f, o, gate: (a * f.astype(jnp.float32) - o.astype(jnp.float32)) * gate
-    grad_x = mix(fx[0], ox[0], here)
-    grad_y = mix(fy[0], oy[0], here)
-    side = grad_x.shape[0]
-    left = mix(fx_l[0], ox_l[0], before)[:, 127:128]
-    right = mix(fx_r[0], ox_r[0], after)[:, 0:1]
-    up = mix(fy_u[0], oy_u[0], above)[15:16, :]
-    down = mix(fy_d[0], oy_d[0], below)[0:1, :]
-    row = lax.broadcasted_iota(jnp.int32, grad_x.shape, 0)
-    col = lax.broadcasted_iota(jnp.int32, grad_x.shape, 1)
-    y_above = jnp.where(row == 0, up, pltpu.roll(grad_y, 1, 0))
-    y_below = jnp.where(row == side - 1, down, pltpu.roll(grad_y, side - 1, 0))
-    x_before = jnp.where(col == 0, left, pltpu.roll(grad_x, 1, 1))
-    x_after = jnp.where(col == side - 1, right, pltpu.roll(grad_x, side - 1, 1))
-    out[0] = (x_before - x_after) * 0.5 + (y_above - y_below) * 0.5
+    side = out.shape[1]
+    chunks = side // CHUNK
+    row = lax.broadcasted_iota(jnp.int32, (CHUNK, side), 0)
+    col = lax.broadcasted_iota(jnp.int32, (CHUNK, side), 1)
+    rows_of = lambda j: pl.ds(pl.multiple_of(j * CHUNK, CHUNK), CHUNK)
+    grad_y = lambda j: mix(fy[0, rows_of(j), :], oy[0, rows_of(j), :], here)
+    top = mix(fy_u[0], oy_u[0], above)[15:16, :]
+    bottom = mix(fy_d[0], oy_d[0], below)[0:1, :]
+
+    def part(j, carry):
+        higher, y = carry
+        at = rows_of(j)
+        x = mix(fx[0, at, :], ox[0, at, :], here)
+        left = mix(fx_l[0, at, :], ox_l[0, at, :], before)[:, 127:128]
+        right = mix(fx_r[0, at, :], ox_r[0, at, :], after)[:, 0:1]
+        y_next = grad_y(jnp.minimum(j + 1, chunks - 1))
+        lower = jnp.where(j == chunks - 1, bottom, y_next[0:1, :])
+        y_above = jnp.where(row == 0, higher, pltpu.roll(y, 1, 0))
+        y_below = jnp.where(row == CHUNK - 1, lower, pltpu.roll(y, CHUNK - 1, 0))
+        x_before = jnp.where(col == 0, left, pltpu.roll(x, 1, 1))
+        x_after = jnp.where(col == side - 1, right, pltpu.roll(x, side - 1, 1))
+        out[0, at, :] = (x_before - x_after) * 0.5 + (y_above - y_below) * 0.5
+        return y[CHUNK - 1 : CHUNK, :], y_next
+
+    lax.fori_loop(0, chunks, part, (top, grad_y(0)), unroll=2)
     lane = lax.broadcasted_iota(jnp.int32, (1, side), 1)
 
     def shot(n, carry):

time: 418 us -> 475 us (1.14)
  Pallas kernels: 402 us -> 461 us
    pallas_call x2, Pallas kernels: 101 us -> 137 us  [image_sums(): pl.pallas_call(functools.partial(image_kernel, rows, cols), out_shape=[fi...]
    pallas_call x2, Pallas kernels: 65.1 us -> 87.6 us  [data_part(): pl.pallas_call(functools.partial(data_kernel, rows, cols), out_shape=jax....]
where the time goes in v4:
time: 475 us; the launch traced here: 474 us
  Pallas kernels  461 us (97%)
  other arithmetic  9.03 us (2%)
    pallas_call x2, Pallas kernels, image_sums(): pl.pallas_call(functools.partial(image_kernel, rows, cols), out_shape=[fi...  137 us
    pallas_call x2, Pallas kernels, gather(): pl.pallas_call(functools.partial(gather_kernel, rows, cols, count), out_s...  127 us
    pallas_call x2, Pallas kernels, data_part(): pl.pallas_call(functools.partial(data_kernel, rows, cols), out_shape=jax....  87.6 us
    pallas_call x2, Pallas kernels, add_parts(): pl.pallas_call(functools.partial(add_kernel, rows, cols), out_shape=jax.S...  72 us
    pallas_call x2, Pallas kernels, total_over_devices(): pl.pallas_call(functools.partial(total_kernel, rows, cols), out_shape=jax...  31.9 us

profile of v4, /device:TPU:0, one launch (start us, length us, event | category | flops | bytes accessed | tf_op | source)
XLA Modules:
  0.0 473.7 jit_solution(17447122639105380698)
XLA Ops:
  0.0 0.8 fusion.4
  0.8 0.1 convert_reduce_fusion.4
  0.9 0.0 copy-start
  0.9 0.8 convert_reduce_fusion.3
  1.7 0.7 select_reduce_fusion.3.start
  2.4 0.7 select_reduce_fusion.4.tile
  3.1 1.6 subtract_convert_fusion.refs_1_
  4.7 74.1 %gather.2 = (f32[2,2,4,2,256,256]{5,4,3,2,1,0:T(8,128)}, bf16[2,2,4,2,256,256]{5,4,3,2,1,0:T(8,128)(2,1)}) custom-call(f32[256,256]{1,0:T(8,128)} %refs_0_.1, bf16[256,256]{1,0:T(8,128)(2,1)} %subtract_convert_fusion.refs_1_), custom_call_target="tpu_custom_call" | custom-call | tf_op jit(solution)/shard_map/gather/pallas_call | solution.py:624
  78.9 0.9 convert_reduce_fusion.2
  79.8 0.7 select_reduce_fusion.2.order
  80.5 0.8 copy.10
  81.2 0.6 reshape.46.sun
  81.9 0.0 copy-start.1
  81.9 0.0 copy-start.2
  81.9 0.0 copy-start.3
  81.9 68.8 %image_sums.2 = (bf16[32,256,256]{2,1,0:T(8,128)(2,1)}, bf16[32,256,256]{2,1,0:T(8,128)(2,1)}, bf16[32,256,256]{2,1,0:T(8,128)(2,1)}, bf16[32,256,256]{2,1,0:T(8,128)(2,1)}, f32[16,128]{1,0:T(8,128)}) custom-call(s32[64]{0:T(128)} %select_reduce_fusion.2.order, s32[32]{0:T(128)} %select_reduce_fusion.4.tile, s32[33]{0:T(128)} %select_reduce_fusion.3.start, ...), custom_call_target="tpu_custom_call" | custom-call | tf_op jit(solution)/shard_map/image_sums/pallas_call | solution.py:180
  150.6 0.0 copy-done
  150.7 18.4 %total.2 = f32[8,128]{1,0:T(8,128)} custom-call(f32[16,128]{1,0:T(8,128)} %get-tuple-element.19.part), custom_call_target="tpu_custom_call" | custom-call | tf_op jit(solution)/shard_map/total/pallas_call | solution.py:356
  169.0 1.2 slice.10
  170.2 0.6 convert_element_type.24.seen
  170.8 0.0 copy-done.1
  170.8 0.2 convert_reduce_fusion
  171.0 0.0 copy-done.2
  171.0 0.7 select_reduce_fusion.shot_height
  171.6 0.0 copy-done.3
  171.6 0.6 select_reduce_fusion.1.shot_pixel
  172.3 0.7 convert_reduce_fusion.1.shot_start
  173.0 43.8 %data_part.2 = f32[32,256,256]{2,1,0:T(8,128)} custom-call(s32[32]{0:T(128)} %copy-done, s32[32]{0:T(128)} %convert_element_type.24.seen, f32[1]{0:T(128)} %bitcast.4.albedo, s32[33]{0:T(128)} %convert_reduce_fusion.1.shot_start, s32[256]{0:T(256)} %select_reduce_fusion.1.shot_pixel, f32[256]{0:T(256)} %select_reduce_fusion.shot_height, ...), custom_call_target="tpu_custom_call" | custom-call | tf_op jit(solution)/shard_map/data_part/pallas_call | solution.py:260
  216.8 35.6 %add_parts.2.data = f32[256,256]{1,0:T(8,128)} custom-call(f32[2,2,4,2,256,256]{5,4,3,2,1,0:T(8,128)} %bitcast.34), custom_call_target="tpu_custom_call" | custom-call | tf_op jit(solution)/shard_map/add_parts/pallas_call | solution.py:499
  252.4 2.2 update.2.refs_0_
  254.6 53.4 %gather.3 = f32[2,2,4,2,256,256]{5,4,3,2,1,0:T(8,128)} custom-call(f32[256,256]{1,0:T(8,128)} %update.2.refs_0_), custom_call_target="tpu_custom_call" | custom-call | tf_op jit(solution)/shard_map/gather/pallas_call | solution.py:624
  308.0 68.7 %image_sums.3 = (bf16[32,256,256]{2,1,0:T(8,128)(2,1)}, bf16[32,256,256]{2,1,0:T(8,128)(2,1)}, bf16[32,256,256]{2,1,0:T(8,128)(2,1)}, bf16[32,256,256]{2,1,0:T(8,128)(2,1)}, f32[16,128]{1,0:T(8,128)}) custom-call(s32[64]{0:T(128)} %select_reduce_fusion.2.order, s32[32]{0:T(128)} %select_reduce_fusion.4.tile, s32[33]{0:T(128)} %select_reduce_fusion.3.start, ...), custom_call_target="tpu_custom_call" | custom-call | tf_op jit(solution)/shard_map/image_sums/pallas_call | solution.py:180
  376.6 13.5 %total.3 = f32[8,128]{1,0:T(8,128)} custom-call(f32[16,128]{1,0:T(8,128)} %get-tuple-element.24.part), custom_call_target="tpu_custom_call" | custom-call | tf_op jit(solution)/shard_map/total/pallas_call | solution.py:356
  390.2 1.2 slice.11
  391.3 43.8 %data_part.3 = f32[32,256,256]{2,1,0:T(8,128)} custom-call(s32[32]{0:T(128)} %copy-done, s32[32]{0:T(128)} %convert_element_type.24.seen, f32[1]{0:T(128)} %bitcast.8.albedo, s32[33]{0:T(128)} %convert_reduce_fusion.1.shot_start, s32[256]{0:T(256)} %select_reduce_fusion.1.shot_pixel, f32[256]{0:T(256)} %select_reduce_fusion.shot_height, ...), custom_call_target="tpu_custom_call" | custom-call | tf_op jit(solution)/shard_map/data_part/pallas_call | solution.py:260
  435.2 36.3 %add_parts.3.data = f32[256,256]{1,0:T(8,128)} custom-call(f32[2,2,4,2,256,256]{5,4,3,2,1,0:T(8,128)} %bitcast.33), custom_call_target="tpu_custom_call" | custom-call | tf_op jit(solution)/shard_map/add_parts/pallas_call | solution.py:499
  471.5 2.2 update.3
  (2 shorter events, 0.0 us)
Async XLA Ops:
  0.9 149.7 %copy-start = (s32[32]{0:T(128)}, s32[32]{0:T(128)S(1)}, u32[]{:S(2)}) copy-start(s32[32]{0:T(128)S(1)} %broadcast_select_fusion.slot) | copy-start | bytes 388
  81.9 88.9 %copy-start.1 = (s32[256,1]{0,1:T(1,128)S(1)}, s32[256,1]{0,1:T(1,128)}, u32[]{:S(2)}) copy-start(s32[256,1]{0,1:T(1,128)} %param.13) | copy-start | bytes 3076
  81.9 89.1 %copy-start.2 = (f32[256]{0:T(256)S(1)}, f32[256]{0:T(256)}, u32[]{:S(2)}) copy-start(f32[256]{0:T(256)} %param.15) | copy-start | bytes 3076
  81.9 89.8 %copy-start.3 = (s32[256]{0:T(256)S(1)}, s32[256]{0:T(256)}, u32[]{:S(2)}) copy-start(s32[256]{0:T(256)} %param.14) | copy-start | bytes 3076

commit v5 on v3

--- a/solution.py
+++ b/solution.py
@@ -119,7 +119,7 @@
         )
         zero = jnp.zeros((CHUNK, side), jnp.float32)
         sums = lax.fori_loop(
-            0, side // CHUNK, functools.partial(step, fresh, numbers), (zero, zero), unroll=2
+            0, side // CHUNK, functools.partial(step, fresh, numbers), (zero, zero), unroll=8
         )
         cross[...] += sums[0]
         power[...] += sums[1]

time: 418 us -> 413 us (0.988)
    pallas_call x2, Pallas kernels: 101 us -> 96.5 us  [image_sums(): pl.pallas_call(functools.partial(image_kernel, rows, cols), out_shape=[fi...]
where the time goes in v5:
time: 413 us; the launch traced here: 411 us
  Pallas kernels  398 us (96%)
  other arithmetic  9.03 us (2%)
    pallas_call x2, Pallas kernels, gather(): pl.pallas_call(functools.partial(gather_kernel, rows, cols, count), out_s...  127 us
    pallas_call x2, Pallas kernels, image_sums(): pl.pallas_call(functools.partial(image_kernel, rows, cols), out_shape=[fi...  96.5 us
    pallas_call x2, Pallas kernels, add_parts(): pl.pallas_call(functools.partial(add_kernel, rows, cols), out_shape=jax.S...  71.7 us
    pallas_call x2, Pallas kernels, data_part(): pl.pallas_call(functools.partial(data_kernel, rows, cols), out_shape=jax....  65.2 us
    pallas_call x2, Pallas kernels, total_over_devices(): pl.pallas_call(functools.partial(total_kernel, rows, cols), out_shape=jax...  32.8 us

profile of v5, /device:TPU:0, one launch (start us, length us, event | category | flops | bytes accessed | tf_op | source)
XLA Modules:
  0.0 410.6 jit_solution(9495177545026056287)
XLA Ops:
  0.0 0.8 fusion.4
  0.8 0.1 convert_reduce_fusion.4
  0.9 0.0 copy-start
  0.9 0.8 convert_reduce_fusion.3
  1.7 0.7 select_reduce_fusion.3.start
  2.4 0.7 select_reduce_fusion.4.tile
  3.1 1.6 subtract_convert_fusion.refs_1_
  4.7 74.1 %gather.2 = (f32[2,2,4,2,256,256]{5,4,3,2,1,0:T(8,128)}, bf16[2,2,4,2,256,256]{5,4,3,2,1,0:T(8,128)(2,1)}) custom-call(f32[256,256]{1,0:T(8,128)} %refs_0_.1, bf16[256,256]{1,0:T(8,128)(2,1)} %subtract_convert_fusion.refs_1_), custom_call_target="tpu_custom_call" | custom-call | tf_op jit(solution)/shard_map/gather/pallas_call | solution.py:595
  78.9 0.9 convert_reduce_fusion.2
  79.8 0.7 select_reduce_fusion.2.order
  80.5 0.8 copy.10
  81.2 0.6 reshape.46.sun
  81.9 0.0 copy-start.1
  81.9 0.0 copy-start.2
  81.9 0.0 copy-start.3
  81.9 48.3 %image_sums.2 = (bf16[32,256,256]{2,1,0:T(8,128)(2,1)}, bf16[32,256,256]{2,1,0:T(8,128)(2,1)}, bf16[32,256,256]{2,1,0:T(8,128)(2,1)}, bf16[32,256,256]{2,1,0:T(8,128)(2,1)}, f32[16,128]{1,0:T(8,128)}) custom-call(s32[64]{0:T(128)} %select_reduce_fusion.2.order, s32[32]{0:T(128)} %select_reduce_fusion.4.tile, s32[33]{0:T(128)} %select_reduce_fusion.3.start, ...), custom_call_target="tpu_custom_call" | custom-call | tf_op jit(solution)/shard_map/image_sums/pallas_call | solution.py:162
  130.2 0.0 copy-done
  130.2 18.4 %total.2 = f32[8,128]{1,0:T(8,128)} custom-call(f32[16,128]{1,0:T(8,128)} %get-tuple-element.19.part), custom_call_target="tpu_custom_call" | custom-call | tf_op jit(solution)/shard_map/total/pallas_call | solution.py:327
  148.6 1.2 slice.10
  149.8 0.6 convert_element_type.24.seen
  150.3 0.0 copy-done.1
  150.3 0.2 convert_reduce_fusion
  150.5 0.0 copy-done.2
  150.5 0.7 select_reduce_fusion.shot_height
  151.2 0.0 copy-done.3
  151.2 0.6 select_reduce_fusion.1.shot_pixel
  151.8 0.7 convert_reduce_fusion.1.shot_start
  152.5 32.6 %data_part.2 = f32[32,256,256]{2,1,0:T(8,128)} custom-call(s32[32]{0:T(128)} %copy-done, s32[32]{0:T(128)} %convert_element_type.24.seen, f32[1]{0:T(128)} %bitcast.4.albedo, s32[33]{0:T(128)} %convert_reduce_fusion.1.shot_start, s32[256]{0:T(256)} %select_reduce_fusion.1.shot_pixel, f32[256]{0:T(256)} %select_reduce_fusion.shot_height, ...), custom_call_target="tpu_custom_call" | custom-call | tf_op jit(solution)/shard_map/data_part/pallas_call | solution.py:231
  185.1 35.6 %add_parts.2.data = f32[256,256]{1,0:T(8,128)} custom-call(f32[2,2,4,2,256,256]{5,4,3,2,1,0:T(8,128)} %bitcast.34), custom_call_target="tpu_custom_call" | custom-call | tf_op jit(solution)/shard_map/add_parts/pallas_call | solution.py:470
  220.8 2.2 update.2.refs_0_
  223.0 52.9 %gather.3 = f32[2,2,4,2,256,256]{5,4,3,2,1,0:T(8,128)} custom-call(f32[256,256]{1,0:T(8,128)} %update.2.refs_0_), custom_call_target="tpu_custom_call" | custom-call | tf_op jit(solution)/shard_map/gather/pallas_call | solution.py:595
  275.9 48.2 %image_sums.3 = (bf16[32,256,256]{2,1,0:T(8,128)(2,1)}, bf16[32,256,256]{2,1,0:T(8,128)(2,1)}, bf16[32,256,256]{2,1,0:T(8,128)(2,1)}, bf16[32,256,256]{2,1,0:T(8,128)(2,1)}, f32[16,128]{1,0:T(8,128)}) custom-call(s32[64]{0:T(128)} %select_reduce_fusion.2.order, s32[32]{0:T(128)} %select_reduce_fusion.4.tile, s32[33]{0:T(128)} %select_reduce_fusion.3.start, ...), custom_call_target="tpu_custom_call" | custom-call | tf_op jit(solution)/shard_map/image_sums/pallas_call | solution.py:162
  324.1 14.4 %total.3 = f32[8,128]{1,0:T(8,128)} custom-call(f32[16,128]{1,0:T(8,128)} %get-tuple-element.24.part), custom_call_target="tpu_custom_call" | custom-call | tf_op jit(solution)/shard_map/total/pallas_call | solution.py:327
  338.5 1.2 slice.11
  339.7 32.6 %data_part.3 = f32[32,256,256]{2,1,0:T(8,128)} custom-call(s32[32]{0:T(128)} %copy-done, s32[32]{0:T(128)} %convert_element_type.24.seen, f32[1]{0:T(128)} %bitcast.8.albedo, s32[33]{0:T(128)} %convert_reduce_fusion.1.shot_start, s32[256]{0:T(256)} %select_reduce_fusion.1.shot_pixel, f32[256]{0:T(256)} %select_reduce_fusion.shot_height, ...), custom_call_target="tpu_custom_call" | custom-call | tf_op jit(solution)/shard_map/data_part/pallas_call | solution.py:231
  372.3 36.1 %add_parts.3.data = f32[256,256]{1,0:T(8,128)} custom-call(f32[2,2,4,2,256,256]{5,4,3,2,1,0:T(8,128)} %bitcast.33), custom_call_target="tpu_custom_call" | custom-call | tf_op jit(solution)/shard_map/add_parts/pallas_call | solution.py:470
  408.4 2.2 update.3
  (2 shorter events, 0.0 us)
Async XLA Ops:
  0.9 129.3 %copy-start = (s32[32]{0:T(128)}, s32[32]{0:T(128)S(1)}, u32[]{:S(2)}) copy-start(s32[32]{0:T(128)S(1)} %broadcast_select_fusion.slot) | copy-start | bytes 388
  81.9 68.5 %copy-start.1 = (s32[256,1]{0,1:T(1,128)S(1)}, s32[256,1]{0,1:T(1,128)}, u32[]{:S(2)}) copy-start(s32[256,1]{0,1:T(1,128)} %param.13) | copy-start | bytes 3076
  81.9 68.7 %copy-start.2 = (f32[256]{0:T(256)S(1)}, f32[256]{0:T(256)}, u32[]{:S(2)}) copy-start(f32[256]{0:T(256)} %param.15) | copy-start | bytes 3076
  81.9 69.3 %copy-start.3 = (s32[256]{0:T(256)S(1)}, s32[256]{0:T(256)}, u32[]{:S(2)}) copy-start(s32[256]{0:T(256)} %param.14) | copy-start | bytes 3076
